TPU v7x, 512 devices: a whole 4x8x8 slice. The times are simulated.
512 devices in a mesh: tm: 8 (over x, core), row: 64 (over z, y).
Axes of the slice: x: 4, y: 8, z: 8, core: 2. Of those that a mesh axis runs over, the one named last changes fastest.
Arguments:
- inputs: bfloat16 [96, 8, 64, 256], P(None, 'tm', 'row'), may hold values from -6 to 6
- cotangent: bfloat16 [96, 8, 64, 256], P(None, 'tm', 'row'), may hold values from -6 to 6
- gain_first: float32 [96], replicated, may hold values from 0.5 to 1.5
- gain_second: float32 [96], replicated, may hold values from 0.5 to 1.5
- bias_first: float32 [96], replicated, may hold values from -3 to 3
- kernel_first: bfloat16 [3, 3, 3, 96, 96], replicated, may hold values from -0.125 to 0.125
- kernel_second: bfloat16 [3, 3, 3, 96, 96], replicated, may hold values from -0.125 to 0.125
Outputs:
- grad_inputs: bfloat16 [96, 8, 64, 256], P(None, 'tm', 'row')
- grad_kernel_first: float32 [3, 3, 3, 96, 96], replicated
- grad_kernel_second: float32 [3, 3, 3, 96, 96], replicated
- grad_vectors: float32 [4, 96], replicated
All inputs are finite; a program needn't handle non-finite values.
Results may differ from a plain program's by a relative error of at most 0.0055.
Values may be sent and summed in bfloat16 or wider, within the bound.
A program may use at most 64 MiB of HBM per device.

v0:
```python
import jax
import jax.numpy as jnp
from jax import lax
from jax.sharding import PartitionSpec as P

epsilon = 1e-06
max_norm = 500.0


def shifted(block, axis, distance):
    devices = range(lax.axis_size(axis))
    route = [(i - distance, i) for i in devices if i - distance in devices]
    return lax.ppermute(block, axis, route)


def extended(block, sides, width):
    for axis, dim in sides:
        count = lax.axis_size(axis)
        forward = [(i, i + 1) for i in range(count - 1)]
        backward = [(target, source) for source, target in forward]
        low = lax.ppermute(
            lax.slice_in_dim(block, block.shape[dim] - width, None, axis=dim), axis, forward
        )
        high = lax.ppermute(lax.slice_in_dim(block, 0, width, axis=dim), axis, backward)
        block = jnp.concatenate([low, block, high], axis=dim)
    return block


def norm_act(values, gain):
    meansq = jnp.mean(values * values, axis=0, keepdims=True)
    scaled = values * lax.rsqrt(meansq + epsilon) * gain.reshape((-1,) + (1,) * (values.ndim - 1))
    return jax.nn.silu(scaled)


def extend(plane, towards):
    frames = [plane]
    for offset in (1, 2):
        frames.append(shifted(plane, "tm", towards * offset))
    ordered = frames[::-1] if towards > 0 else frames
    banded = extended(jnp.stack(ordered, axis=1), (("row", 2),), 1)
    return jnp.pad(banded, ((0, 0), (0, 0), (0, 0), (1, 1)))


def spread(volume, towards):
    return extend(volume[:, 0], towards)


def forward_conv(padded, kernel, frame_count, row_count, col_count):
    total = jnp.zeros((kernel.shape[3], frame_count, row_count, col_count), jnp.float32)
    for tap_t in range(3):
        for tap_h in range(3):
            for tap_w in range(3):
                window = padded[
                    :,
                    tap_t : tap_t + frame_count,
                    tap_h : tap_h + row_count,
                    tap_w : tap_w + col_count,
                ]
                total = total + jnp.einsum(
                    "oc,ctrw->otrw",
                    kernel[tap_t, tap_h, tap_w],
                    window,
                    preferred_element_type=jnp.float32,
                )
    return total


def input_grad(padded, kernel, frame_count, row_count, col_count):
    total = jnp.zeros((kernel.shape[4], frame_count, row_count, col_count), jnp.float32)
    for tap_t in range(3):
        for tap_h in range(3):
            for tap_w in range(3):
                window = padded[
                    :,
                    2 - tap_t : 2 - tap_t + frame_count,
                    2 - tap_h : 2 - tap_h + row_count,
                    2 - tap_w : 2 - tap_w + col_count,
                ]
                total = total + jnp.einsum(
                    "oc,otrw->ctrw",
                    kernel[tap_t, tap_h, tap_w],
                    window,
                    preferred_element_type=jnp.float32,
                )
    return total


def kernel_grad(padded, upstream, frame_count, row_count, col_count):
    pieces = []
    for tap_t in range(3):
        for tap_h in range(3):
            for tap_w in range(3):
                window = padded[
                    :,
                    tap_t : tap_t + frame_count,
                    tap_h : tap_h + row_count,
                    tap_w : tap_w + col_count,
                ]
                pieces.append(
                    jnp.einsum(
                        "otrw,ctrw->oc", upstream, window, preferred_element_type=jnp.float32
                    )
                )
    stacked = jnp.stack(pieces)
    return stacked.reshape((3, 3, 3) + stacked.shape[1:])


def body(inputs, cotangent, gain_first, gain_second, bias_first, kernel_first, kernel_second):
    local_in, local_cot = (inputs, cotangent)
    frame_count = local_in.shape[1]
    row_count = local_in.shape[2]
    col_count = local_in.shape[3]
    input_wide = local_in.astype(jnp.float32)
    first = norm_act(input_wide, gain_first).astype(jnp.bfloat16)
    prior_first = spread(first, 1)
    hidden = (
        forward_conv(prior_first, kernel_first, frame_count, row_count, col_count)
        + bias_first[:, None, None, None]
    )
    second_wide, act_back = jax.vjp(norm_act, hidden, gain_second)
    second = second_wide.astype(jnp.bfloat16)
    grad_second = input_grad(
        spread(local_cot, -1), kernel_second, frame_count, row_count, col_count
    )
    raw_second = kernel_grad(spread(second, 1), local_cot, frame_count, row_count, col_count)
    grad_hidden, raw_gain_second = act_back(grad_second)
    hidden_cot = grad_hidden.astype(jnp.bfloat16)
    grad_first = input_grad(spread(hidden_cot, -1), kernel_first, frame_count, row_count, col_count)
    raw_first = kernel_grad(prior_first, hidden_cot, frame_count, row_count, col_count)
    _, input_back = jax.vjp(norm_act, input_wide, gain_first)
    input_term, raw_gain_first = input_back(grad_first)
    cot_wide = local_cot.astype(jnp.float32)
    grad_local = (cot_wide + input_term).astype(jnp.bfloat16)
    raw_vectors = jnp.stack(
        [
            jnp.sum(grad_hidden, axis=(1, 2, 3)),
            raw_gain_first,
            raw_gain_second,
            jnp.sum(cot_wide, axis=(1, 2, 3)),
        ]
    )
    summed_first, summed_second, summed_vectors = lax.psum(
        (raw_first, raw_second, raw_vectors), ("tm", "row")
    )
    total = jnp.sqrt(
        jnp.sum(summed_first * summed_first)
        + jnp.sum(summed_second * summed_second)
        + jnp.sum(summed_vectors * summed_vectors)
    )
    factor = jnp.minimum(jnp.float32(1.0), max_norm / (total + epsilon))
    grad_kernel_first = summed_first * factor
    grad_kernel_second = summed_second * factor
    return (grad_local, grad_kernel_first, grad_kernel_second, summed_vectors * factor)


def solution(mesh):
    in_specs = (P(None, "tm", "row", None), P(None, "tm", "row", None), P(), P(), P(), P(), P())
    out_specs = (P(None, "tm", "row", None), P(), P(), P())
    return jax.shard_map(body, mesh=mesh, in_specs=in_specs, out_specs=out_specs, check_vma=False)
```

profile of v0, /device:TPU:1, one launch (start us, length us, event | category | flops | bytes accessed | tf_op | source)
XLA Modules:
  0.0 394.6 jit_solution(9914092340614937374)
XLA Ops:
  7.2 0.9 fusion.146
  8.1 0.9 fusion.394
  9.0 4.5 %collective-permute-start.5 = (bf16[96,1,256]{2,0,1:T(8,128)(2,1)S(1)}, bf16[96,1,256]{2,0,1:T(8,128)(2,1)S(1)}, u32[]{:S(2)}, u32[]{:S(2)}) collective-permute-start(bf16[96,1,256]{2,0,1:T(8,128)(2,1)S(1)} %fusion.394), channel_id=1, source_target_pairs={{0,64},{64,128},{128,192},{192,256},{256,320},{320,384},{384,448},... | collective-permute-start | bytes 147464 | tf_op jit(solution)/shard_map/ppermute | solution.py:13
  13.6 3.1 collective-permute-start.4
  16.7 1.3 collective-permute-start.1
  18.0 3.7 collective-permute-start
  21.7 0.9 fusion.139
  22.7 1.3 collective-permute-start.7
  24.0 4.0 %collective-permute-start.6 = (bf16[96,3,1,256]{3,0,2,1:T(8,128)(2,1)S(1)}, bf16[96,3,1,256]{3,0,2,1:T(8,128)(2,1)S(1)}, u32[]{:S(2)}, u32[]{:S(2)}) collective-permute-start(bf16[96,3,1,256]{3,0,2,1:T(8,128)(2,1)S(1)} %pad_maximum_fusion.1), channel_id=1, source_target_pairs={{0,1},{1,2},{2,3},{3,4},{4,5},{5,6},{6,7},{7,8},{8,9},{9,10},{10,1... | collective-permute-start | bytes 442376 | tf_op jit(solution)/shard_map/ppermute | solution.py:21
  28.0 0.9 pad_maximum_fusion
  28.9 1.3 collective-permute-start.3
  30.2 4.0 %collective-permute-start.2 = (bf16[96,3,1,256]{3,0,2,1:T(8,128)(2,1)S(1)}, bf16[96,3,1,256]{3,0,2,1:T(8,128)(2,1)S(1)}, u32[]{:S(2)}, u32[]{:S(2)}) collective-permute-start(bf16[96,3,1,256]{3,0,2,1:T(8,128)(2,1)S(1)} %pad_maximum_fusion), channel_id=1, source_target_pairs={{0,1},{1,2},{2,3},{3,4},{4,5},{5,6},{6,7},{7,8},{8,9},{9,10},{10,1... | collective-permute-start | bytes 442376 | tf_op jit(solution)/shard_map/ppermute | solution.py:21
  34.2 0.3 fusion.126
  36.4 0.9 collective-permute-done.2
  37.2 0.3 fusion.122
  38.2 0.2 convolution_bitcast_fusion.30
  39.1 0.2 convolution_bitcast_fusion.38
  39.5 0.2 fusion.153
  43.1 0.2 fusion.50
  43.8 0.2 fusion.46
  44.3 0.2 fusion.43
  44.9 0.2 fusion.39
  45.4 0.2 fusion.36
  46.0 0.2 fusion.34
  46.3 0.2 multiply_reduce_fusion.3
  46.7 1.3 collective-permute-start.9
  48.0 2.9 collective-permute-start.8
  51.1 4.8 %collective-permute-start.13 = (bf16[96,1,256]{2,0,1:T(8,128)(2,1)S(1)}, bf16[96,1,256]{2,0,1:T(8,128)(2,1)S(1)}, u32[]{:S(2)}, u32[]{:S(2)}) collective-permute-start(bf16[96,1,256]{2,0,1:T(8,128)(2,1)S(1)} %bitcast.1128), channel_id=1, source_target_pairs={{0,64},{64,128},{128,192},{192,256},{256,320},{320,384},{384,448},... | collective-permute-start | bytes 147464 | tf_op jit(solution)/shard_map/ppermute | solution.py:13
  55.9 3.6 collective-permute-start.12
  59.7 0.2 fusion.105
  60.2 0.2 fusion.102
  60.7 0.2 fusion.99
  61.3 0.2 fusion.96
  61.8 0.2 fusion.93
  62.3 0.2 fusion.90
  62.8 0.2 fusion.87
  63.4 0.2 fusion.84
  63.9 1.3 collective-permute-start.11
  65.2 4.7 %collective-permute-start.10 = (bf16[96,3,1,256]{3,0,2,1:T(8,128)(2,1)S(1)}, bf16[96,3,1,256]{3,0,2,1:T(8,128)(2,1)S(1)}, u32[]{:S(2)}, u32[]{:S(2)}) collective-permute-start(bf16[96,3,1,256]{3,0,2,1:T(8,128)(2,1)S(1)} %pad_maximum_fusion.2), channel_id=1, source_target_pairs={{0,1},{1,2},{2,3},{3,4},{4,5},{5,6},{6,7},{7,8},{8,9},{9,10},{10,1... | collective-permute-start | bytes 442376 | tf_op jit(solution)/shard_map/ppermute | solution.py:21
  70.3 1.3 collective-permute-start.15
  71.6 4.0 %collective-permute-start.14 = (bf16[96,3,1,256]{3,0,2,1:T(8,128)(2,1)S(1)}, bf16[96,3,1,256]{3,0,2,1:T(8,128)(2,1)S(1)}, u32[]{:S(2)}, u32[]{:S(2)}) collective-permute-start(bf16[96,3,1,256]{3,0,2,1:T(8,128)(2,1)S(1)} %pad_maximum_fusion.3), channel_id=1, source_target_pairs={{0,1},{1,2},{2,3},{3,4},{4,5},{5,6},{6,7},{7,8},{8,9},{9,10},{10,1... | collective-permute-start | bytes 442376 | tf_op jit(solution)/shard_map/ppermute | solution.py:21
  75.6 0.3 select_maximum_fusion.4
  77.2 0.2 fusion.152
  77.9 0.2 convolution_add_fusion.21
  78.3 0.2 convolution_add_fusion.19
  78.8 0.2 convolution_add_fusion.17
  79.2 0.2 convolution_add_fusion.15
  79.7 0.2 convolution_add_fusion.13
  80.1 0.2 fusion.25
  80.6 0.2 fusion.22
  81.3 0.2 fusion.19
  81.5 0.3 select_maximum_fusion
  86.4 1.5 copy.11
  88.1 0.6 copy-done.5
  88.7 0.3 fusion.142
  89.0 0.8 convert_reduce_fusion
  89.8 112.1 %psum.23 = f32[4,96]{1,0:T(4,128)S(1)} all-reduce(f32[4,96]{1,0:T(4,128)S(1)} %pad_maximum_fusion.4), channel_id=1, replica_groups=mesh['tm'=8,'row'=64] {'tm','row'}, use_global_device_ids=true, to_apply=%region_12.13 | all-reduce | flops 384 | bytes 3072 | tf_op jit(solution)/shard_map/psum | solution.py:142
  201.9 0.6 multiply_reduce_fusion.5
  202.5 177.0 %all-reduce.7.cloned.1.call-done = (f32[3,3,3,96,96]{4,3,2,1,0:T(8,128)}, f32[3,3,3,96,96]{4,3,2,1,0:T(8,128)}) async-done(((f32[3,3,3,96,96]{4,3,2,1,0:T(8,128)}, f32[3,3,3,96,96]{4,3,2,1,0:T(8,128)}), (f32[3,3,3,96,96]{4,3,2,1,0:T(8,128)}, f32[3,3,3,96,96]{4,3,2,1,0:T(8,128)})) %all-reduce.7.cloned.1.call-update) | async-done | bytes 1990672 | tf_op jit(solution)/shard_map/psum | solution.py:142
  379.5 2.8 multiply_reduce_fusion
  384.3 1.2 broadcast_multiply_fusion.1
  385.4 0.6 copy-done.1
  386.1 1.2 broadcast_multiply_fusion
  387.2 0.6 broadcast_multiply_fusion.2
  (151 shorter events, 19.2 us)
Async XLA Ops:
  7.2 27.4 %copy-start.3 = (bf16[3,3,3,96,96]{4,3,2,1,0:T(8,128)(2,1)S(1)}, bf16[3,3,3,96,96]{4,3,2,1,0:T(8,128)(2,1)}, u32[]{:S(2)}) copy-start(bf16[3,3,3,96,96]{4,3,2,1,0:T(8,128)(2,1)} %param.12) | copy-start | bytes 1492996
  7.2 372.4 %all-reduce.7.cloned.1.call-start = ((), (), s32[]{:S(2)}) async-start(), calls=%async_computation | async-start | bytes 5308416 | tf_op jit(solution)/shard_map/psum | solution.py:142
  9.0 13.6 %collective-permute-start.5 = (bf16[96,1,256]{2,0,1:T(8,128)(2,1)S(1)}, bf16[96,1,256]{2,0,1:T(8,128)(2,1)S(1)}, u32[]{:S(2)}, u32[]{:S(2)}) collective-permute-start(bf16[96,1,256]{2,0,1:T(8,128)(2,1)S(1)} %fusion.394), channel_id=1, source_target_pairs={{0,64},{64,128},{128,192},{192,256},{256,320},{320,384},{384,448},... | collective-permute-start | bytes 147464 | tf_op jit(solution)/shard_map/ppermute | solution.py:13
  13.6 9.1 %collective-permute-start.4 = (bf16[96,1,256]{2,0,1:T(8,128)(2,1)S(1)}, bf16[96,1,256]{2,0,1:T(8,128)(2,1)S(1)}, u32[]{:S(2)}, u32[]{:S(2)}) collective-permute-start(bf16[96,1,256]{2,0,1:T(8,128)(2,1)S(1)} %fusion.394), channel_id=1, source_target_pairs={{0,128},{64,192},{128,256},{192,320},{256,384},{320,448},{1,129},{... | collective-permute-start | bytes 147464 | tf_op jit(solution)/shard_map/ppermute | solution.py:13
  16.7 11.3 %collective-permute-start.1 = (bf16[96,1,256]{2,0,1:T(8,128)(2,1)}, bf16[96,1,256]{2,0,1:T(8,128)(2,1)S(1)}, u32[]{:S(2)}, u32[]{:S(2)}) collective-permute-start(bf16[96,1,256]{2,0,1:T(8,128)(2,1)} %bitcast.1120), channel_id=1, source_target_pairs={{128,0},{192,64},{256,128},{320,192},{384,256},{448,320},{129,1},{... | collective-permute-start | bytes 147464 | tf_op jit(solution)/shard_map/ppermute | solution.py:13
  18.0 10.0 %collective-permute-start = (bf16[96,1,256]{2,0,1:T(8,128)(2,1)}, bf16[96,1,256]{2,0,1:T(8,128)(2,1)S(1)}, u32[]{:S(2)}, u32[]{:S(2)}) collective-permute-start(bf16[96,1,256]{2,0,1:T(8,128)(2,1)} %bitcast.1121), channel_id=1, source_target_pairs={{64,0},{128,64},{192,128},{256,192},{320,256},{384,320},{448,384},... | collective-permute-start | bytes 147464 | tf_op jit(solution)/shard_map/ppermute | solution.py:13
  22.7 11.5 %collective-permute-start.7 = (bf16[96,3,1,256]{3,0,2,1:T(8,128)(2,1)S(1)}, bf16[96,3,1,256]{3,0,2,1:T(8,128)(2,1)S(1)}, u32[]{:S(2)}, u32[]{:S(2)}) collective-permute-start(bf16[96,3,1,256]{3,0,2,1:T(8,128)(2,1)S(1)} %pad_maximum_fusion.1), channel_id=1, source_target_pairs={{1,0},{2,1},{3,2},{4,3},{5,4},{6,5},{7,6},{8,7},{9,8},{10,9},{11,1... | collective-permute-start | bytes 442376 | tf_op jit(solution)/shard_map/ppermute | solution.py:24
  24.0 10.2 %collective-permute-start.6 = (bf16[96,3,1,256]{3,0,2,1:T(8,128)(2,1)S(1)}, bf16[96,3,1,256]{3,0,2,1:T(8,128)(2,1)S(1)}, u32[]{:S(2)}, u32[]{:S(2)}) collective-permute-start(bf16[96,3,1,256]{3,0,2,1:T(8,128)(2,1)S(1)} %pad_maximum_fusion.1), channel_id=1, source_target_pairs={{0,1},{1,2},{2,3},{3,4},{4,5},{5,6},{6,7},{7,8},{8,9},{9,10},{10,1... | collective-permute-start | bytes 442376 | tf_op jit(solution)/shard_map/ppermute | solution.py:21
  28.0 9.2 %copy-start = (bf16[96,1,1,256]{3,0,2,1:T(8,128)(2,1)S(1)}, bf16[96,1,1,256]{3,0,2,1:T(8,128)(2,1)}, u32[]{:S(2)}) copy-start(bf16[96,1,1,256]{3,0,2,1:T(8,128)(2,1)} %param.8) | copy-start | bytes 147460
  28.9 7.4 %collective-permute-start.3 = (bf16[96,3,1,256]{3,0,2,1:T(8,128)(2,1)S(1)}, bf16[96,3,1,256]{3,0,2,1:T(8,128)(2,1)S(1)}, u32[]{:S(2)}, u32[]{:S(2)}) collective-permute-start(bf16[96,3,1,256]{3,0,2,1:T(8,128)(2,1)S(1)} %pad_maximum_fusion), channel_id=1, source_target_pairs={{1,0},{2,1},{3,2},{4,3},{5,4},{6,5},{7,6},{8,7},{9,8},{10,9},{11,1... | collective-permute-start | bytes 442376 | tf_op jit(solution)/shard_map/ppermute | solution.py:24
  30.2 7.0 %collective-permute-start.2 = (bf16[96,3,1,256]{3,0,2,1:T(8,128)(2,1)S(1)}, bf16[96,3,1,256]{3,0,2,1:T(8,128)(2,1)S(1)}, u32[]{:S(2)}, u32[]{:S(2)}) collective-permute-start(bf16[96,3,1,256]{3,0,2,1:T(8,128)(2,1)S(1)} %pad_maximum_fusion), channel_id=1, source_target_pairs={{0,1},{1,2},{2,3},{3,4},{4,5},{5,6},{6,7},{7,8},{8,9},{9,10},{10,1... | collective-permute-start | bytes 442376 | tf_op jit(solution)/shard_map/ppermute | solution.py:21
  34.6 3.0 copy-start.6
  41.1 1.4 copy-start.8
  44.5 1.8 copy-start.9
  46.7 17.2 %collective-permute-start.9 = (bf16[96,1,256]{2,0,1:T(8,128)(2,1)S(1)}, bf16[96,1,256]{2,0,1:T(8,128)(2,1)S(1)}, u32[]{:S(2)}, u32[]{:S(2)}) collective-permute-start(bf16[96,1,256]{2,0,1:T(8,128)(2,1)S(1)} %bitcast.1122), channel_id=1, source_target_pairs={{128,0},{192,64},{256,128},{320,192},{384,256},{448,320},{129,1},{... | collective-permute-start | bytes 147464 | tf_op jit(solution)/shard_map/ppermute | solution.py:13
  48.0 15.9 %collective-permute-start.8 = (bf16[96,1,256]{2,0,1:T(8,128)(2,1)S(1)}, bf16[96,1,256]{2,0,1:T(8,128)(2,1)S(1)}, u32[]{:S(2)}, u32[]{:S(2)}) collective-permute-start(bf16[96,1,256]{2,0,1:T(8,128)(2,1)S(1)} %bitcast.1123), channel_id=1, source_target_pairs={{64,0},{128,64},{192,128},{256,192},{320,256},{384,320},{448,384},... | collective-permute-start | bytes 147464 | tf_op jit(solution)/shard_map/ppermute | solution.py:13
  51.1 19.1 %collective-permute-start.13 = (bf16[96,1,256]{2,0,1:T(8,128)(2,1)S(1)}, bf16[96,1,256]{2,0,1:T(8,128)(2,1)S(1)}, u32[]{:S(2)}, u32[]{:S(2)}) collective-permute-start(bf16[96,1,256]{2,0,1:T(8,128)(2,1)S(1)} %bitcast.1128), channel_id=1, source_target_pairs={{0,64},{64,128},{128,192},{192,256},{256,320},{320,384},{384,448},... | collective-permute-start | bytes 147464 | tf_op jit(solution)/shard_map/ppermute | solution.py:13
  55.9 14.3 %collective-permute-start.12 = (bf16[96,1,256]{2,0,1:T(8,128)(2,1)S(1)}, bf16[96,1,256]{2,0,1:T(8,128)(2,1)S(1)}, u32[]{:S(2)}, u32[]{:S(2)}) collective-permute-start(bf16[96,1,256]{2,0,1:T(8,128)(2,1)S(1)} %bitcast.1129), channel_id=1, source_target_pairs={{0,128},{64,192},{128,256},{192,320},{256,384},{320,448},{1,129},{... | collective-permute-start | bytes 147464 | tf_op jit(solution)/shard_map/ppermute | solution.py:13
  63.9 11.6 %collective-permute-start.11 = (bf16[96,3,1,256]{3,0,2,1:T(8,128)(2,1)S(1)}, bf16[96,3,1,256]{3,0,2,1:T(8,128)(2,1)S(1)}, u32[]{:S(2)}, u32[]{:S(2)}) collective-permute-start(bf16[96,3,1,256]{3,0,2,1:T(8,128)(2,1)S(1)} %pad_maximum_fusion.2), channel_id=1, source_target_pairs={{1,0},{2,1},{3,2},{4,3},{5,4},{6,5},{7,6},{8,7},{9,8},{10,9},{11,1... | collective-permute-start | bytes 442376 | tf_op jit(solution)/shard_map/ppermute | solution.py:24
  65.2 10.3 %collective-permute-start.10 = (bf16[96,3,1,256]{3,0,2,1:T(8,128)(2,1)S(1)}, bf16[96,3,1,256]{3,0,2,1:T(8,128)(2,1)S(1)}, u32[]{:S(2)}, u32[]{:S(2)}) collective-permute-start(bf16[96,3,1,256]{3,0,2,1:T(8,128)(2,1)S(1)} %pad_maximum_fusion.2), channel_id=1, source_target_pairs={{0,1},{1,2},{2,3},{3,4},{4,5},{5,6},{6,7},{7,8},{8,9},{9,10},{10,1... | collective-permute-start | bytes 442376 | tf_op jit(solution)/shard_map/ppermute | solution.py:21
  70.2 7.4 %copy-start.4 = (f32[27,96,96]{2,1,0:T(8,128)}, f32[27,96,96]{2,1,0:T(8,128)S(1)}, u32[]{:S(2)}) copy-start(f32[27,96,96]{2,1,0:T(8,128)S(1)} %fusion.81) | copy-start | bytes 2985988
  70.3 11.2 %collective-permute-start.15 = (bf16[96,3,1,256]{3,0,2,1:T(8,128)(2,1)S(1)}, bf16[96,3,1,256]{3,0,2,1:T(8,128)(2,1)S(1)}, u32[]{:S(2)}, u32[]{:S(2)}) collective-permute-start(bf16[96,3,1,256]{3,0,2,1:T(8,128)(2,1)S(1)} %pad_maximum_fusion.3), channel_id=1, source_target_pairs={{1,0},{2,1},{3,2},{4,3},{5,4},{6,5},{7,6},{8,7},{9,8},{10,9},{11,1... | collective-permute-start | bytes 442376 | tf_op jit(solution)/shard_map/ppermute | solution.py:24
  71.6 9.9 %collective-permute-start.14 = (bf16[96,3,1,256]{3,0,2,1:T(8,128)(2,1)S(1)}, bf16[96,3,1,256]{3,0,2,1:T(8,128)(2,1)S(1)}, u32[]{:S(2)}, u32[]{:S(2)}) collective-permute-start(bf16[96,3,1,256]{3,0,2,1:T(8,128)(2,1)S(1)} %pad_maximum_fusion.3), channel_id=1, source_target_pairs={{0,1},{1,2},{2,3},{3,4},{4,5},{5,6},{6,7},{7,8},{8,9},{9,10},{10,1... | collective-permute-start | bytes 442376 | tf_op jit(solution)/shard_map/ppermute | solution.py:21
  87.9 0.8 copy-start.5
  87.9 0.8 copy-start.7
  379.5 4.7 %copy-start.2 = (f32[3,3,3,96,96]{4,3,2,1,0:T(8,128)S(1)}, f32[3,3,3,96,96]{4,3,2,1,0:T(8,128)}, u32[]{:S(2)}) copy-start(f32[3,3,3,96,96]{4,3,2,1,0:T(8,128)} %get-tuple-element.8) | copy-start | bytes 2985988
  384.3 1.8 copy-start.1
Sparse Core Ops, SparseCore 0:
  88.0 291.4 all-reduce.6
where the time goes:
time: 396 us; the launch traced here: 395 us
  waiting for transfers between devices  178 us (45%)
  blocking collectives  112 us (28%)
  starting transfers between devices  47.3 us (12%)
  matrix products  25.2 us (6%)
  between operations  16.9 us (4%)
  other arithmetic  12.3 us (3%)
    psum x1, waiting for transfers between devices, body(): lax.psum((raw_first, raw_second, raw_vectors), ('tm', 'row'))  177 us
    psum x1, blocking collectives, body(): lax.psum((raw_first, raw_second, raw_vectors), ('tm', 'row'))  112 us
    ppermute x8, starting transfers between devices, shifted(): return lax.ppermute(block, axis, route)  25.3 us
    ppermute x4, starting transfers between devices, extended(): lax.ppermute(lax.slice_in_dim(block, block.shape[dim] - width, None, axis...  16.7 us
    dot_general x54, matrix products, input_grad(): jnp.einsum('oc,otrw->ctrw', kernel[tap_t, tap_h, tap_w], window, preferre...  11.7 us
    dot_general x54, matrix products, kernel_grad(): jnp.einsum('otrw,ctrw->oc', upstream, window, preferred_element_type=jnp....  9.13 us
  transfers between devices with their start and end apart: 17, of which 3 were waited for; matrix products, arithmetic and copies ran while one was open for 4% of the time, Pallas kernels for 0%

commit v1 on v0

--- a/solution.py
+++ b/solution.py
@@ -1,6 +1,8 @@
 import jax
 import jax.numpy as jnp
 from jax import lax
+from jax.experimental import pallas as pl
+from jax.experimental.pallas import tpu as pltpu
 from jax.sharding import PartitionSpec as P
 
 epsilon = 1e-06
@@ -105,6 +107,158 @@
     return stacked.reshape((3, 3, 3) + stacked.shape[1:])
 
 
+ROWS_ALL = 4096
+LANES = 128
+MESH = pl.DeviceIdType.MESH
+
+
+def reduce_kernel(z_ref, g_ref, core_in, part, x_out, x_in, y_in, y_own, z_in, z_all,
+                  core_sem, x_sem, y_sem, z_sem, gz_sem, gy_sem, gx_sem, gc_sem):
+    tm, row = lax.axis_index("tm"), lax.axis_index("row")
+    me_x, me_c = tm // 2, tm % 2
+    me_z, me_y = row // 8, row % 8
+    peer_c = {"tm": me_x * 2 + 1 - me_c, "row": row}
+
+    def at_x(d):
+        return lax.rem(me_x + d, 4)
+
+    def at_y(d):
+        return lax.rem(me_y + d, 8)
+
+    def at_z(d):
+        return lax.rem(me_z + d, 8)
+
+    def peer_x(d):
+        return {"tm": at_x(d) * 2 + me_c, "row": row}
+
+    def peer_y(d):
+        return {"tm": tm, "row": me_z * 8 + at_y(d)}
+
+    def peer_z(d):
+        return {"tm": tm, "row": at_z(d) * 8 + me_y}
+
+    def send(src, dst, sems, slot, device):
+        copy = pltpu.make_async_remote_copy(
+            src_ref=src, dst_ref=dst, send_sem=sems.at[0, slot], recv_sem=sems.at[1, slot],
+            device_id=device, device_id_type=MESH,
+        )
+        copy.start()
+        return copy
+
+    barrier = pltpu.get_barrier_semaphore()
+    peers = [peer_c] + [peer_x(d) for d in range(1, 4)]
+    peers += [peer_y(d) for d in range(1, 8)] + [peer_z(d) for d in range(1, 8)]
+    for peer in peers:
+        pl.semaphore_signal(barrier, inc=1, device_id=peer, device_id_type=MESH)
+    pl.semaphore_wait(barrier, len(peers))
+
+    sent = []
+    halves = []
+    for k in range(4):
+        chunk = at_x(k + 1) * 512
+        theirs = pl.ds(pl.multiple_of((1 - me_c) * 2048 + chunk, 512), 512)
+        land = pl.ds(pl.multiple_of(chunk, 512), 512)
+        halves.append(send(z_ref.at[theirs], core_in.at[land], core_sem, k, peer_c))
+    arrivals = []
+    for k in range(4):
+        halves[k].wait_recv()
+        chunk = at_x(k + 1) * 512
+        mine = pl.ds(pl.multiple_of(me_c * 2048 + chunk, 512), 512)
+        land = pl.ds(pl.multiple_of(chunk, 512), 512)
+        total = z_ref[mine, :] + core_in[land, :]
+        if k < 3:
+            x_out[k] = total.astype(jnp.bfloat16)
+            arrivals.append(send(x_out.at[k], x_in.at[k], x_sem, k, peer_x(k + 1)))
+        else:
+            part[...] = total
+    sent += halves + arrivals
+
+    for copy in arrivals:
+        copy.wait_recv()
+    total = part[...]
+    for k in range(3):
+        total = total + x_in[k].astype(jnp.float32)
+    part[...] = total
+    arrivals = []
+    for d in range(1, 8):
+        theirs = pl.ds(pl.multiple_of(at_y(d) * 64, 64), 64)
+        arrivals.append(send(part.at[theirs], y_in.at[d - 1], y_sem, d - 1, peer_y(d)))
+    sent += arrivals
+    for copy in arrivals:
+        copy.wait_recv()
+    total = part[pl.ds(pl.multiple_of(me_y * 64, 64), 64), :]
+    for k in range(7):
+        total = total + y_in[k]
+    y_own[...] = total
+    arrivals = []
+    for d in range(1, 8):
+        theirs = pl.ds(pl.multiple_of(at_z(d) * 8, 8), 8)
+        arrivals.append(send(y_own.at[theirs], z_in.at[d - 1], z_sem, d - 1, peer_z(d)))
+    sent += arrivals
+    for copy in arrivals:
+        copy.wait_recv()
+    own = pl.ds(pl.multiple_of(me_z * 8, 8), 8)
+    total = y_own[own, :]
+    for k in range(7):
+        total = total + z_in[k]
+    z_all[own, :] = total
+    arrivals = []
+    for d in range(1, 8):
+        arrivals.append(send(z_all.at[own], z_all.at[own], gz_sem, d - 1, peer_z(d)))
+    sent += arrivals
+    for copy in arrivals:
+        copy.wait_recv()
+    base = me_c * 2048 + me_x * 512
+    mine = pl.ds(pl.multiple_of(base + me_y * 64, 64), 64)
+    g_ref[mine, :] = z_all[...].astype(jnp.bfloat16)
+    arrivals = []
+    for d in range(1, 8):
+        arrivals.append(send(g_ref.at[mine], g_ref.at[mine], gy_sem, d - 1, peer_y(d)))
+    sent += arrivals
+    for copy in arrivals:
+        copy.wait_recv()
+    mine = pl.ds(pl.multiple_of(base, 512), 512)
+    arrivals = []
+    for d in range(1, 4):
+        arrivals.append(send(g_ref.at[mine], g_ref.at[mine], gx_sem, d - 1, peer_x(d)))
+    cores = [send(g_ref.at[mine], g_ref.at[mine], gc_sem, 0, peer_c)]
+    sent += arrivals
+    for d in range(1, 4):
+        arrivals[d - 1].wait_recv()
+        there = pl.ds(pl.multiple_of(me_c * 2048 + at_x(4 - d) * 512, 512), 512)
+        cores.append(send(g_ref.at[there], g_ref.at[there], gc_sem, d, peer_c))
+    sent += cores
+    for copy in cores:
+        copy.wait_recv()
+    for copy in sent:
+        copy.wait_send()
+
+
+def all_sum(packed):
+    f32, bf16, dma = jnp.float32, jnp.bfloat16, pltpu.SemaphoreType.DMA
+    return pl.pallas_call(
+        reduce_kernel,
+        out_shape=jax.ShapeDtypeStruct((ROWS_ALL, LANES), bf16),
+        in_specs=[pl.BlockSpec(memory_space=pltpu.VMEM)],
+        out_specs=pl.BlockSpec(memory_space=pltpu.VMEM),
+        scratch_shapes=[
+            pltpu.VMEM((2048, LANES), f32),
+            pltpu.VMEM((512, LANES), f32),
+            pltpu.VMEM((3, 512, LANES), bf16),
+            pltpu.VMEM((3, 512, LANES), bf16),
+            pltpu.VMEM((7, 64, LANES), f32),
+            pltpu.VMEM((64, LANES), f32),
+            pltpu.VMEM((7, 8, LANES), f32),
+            pltpu.VMEM((64, LANES), f32),
+            dma((2, 4)), dma((2, 3)), dma((2, 7)), dma((2, 7)),
+            dma((2, 7)), dma((2, 7)), dma((2, 3)), dma((2, 4)),
+        ],
+        compiler_params=pltpu.CompilerParams(
+            collective_id=0, has_side_effects=True, vmem_limit_bytes=40 * 1024 * 1024
+        ),
+    )(packed)
+
+
 def body(inputs, cotangent, gain_first, gain_second, bias_first, kernel_first, kernel_second):
     local_in, local_cot = (inputs, cotangent)
     frame_count = local_in.shape[1]
@@ -139,9 +293,16 @@
             jnp.sum(cot_wide, axis=(1, 2, 3)),
         ]
     )
-    summed_first, summed_second, summed_vectors = lax.psum(
-        (raw_first, raw_second, raw_vectors), ("tm", "row")
-    )
+    sizes = [raw_first.size, raw_second.size, raw_vectors.size]
+    spare = ROWS_ALL * LANES - sum(sizes)
+    flat = jnp.concatenate(
+        [raw_first.reshape(-1), raw_second.reshape(-1), raw_vectors.reshape(-1), jnp.zeros((spare,), jnp.float32)]
+    )
+    flat = all_sum(flat.reshape(ROWS_ALL, LANES)).astype(jnp.float32).reshape(-1)
+    ends = [sizes[0], sizes[0] + sizes[1], sum(sizes)]
+    summed_first = flat[: ends[0]].reshape(raw_first.shape)
+    summed_second = flat[ends[0] : ends[1]].reshape(raw_second.shape)
+    summed_vectors = flat[ends[1] : ends[2]].reshape(raw_vectors.shape)
     total = jnp.sqrt(
         jnp.sum(summed_first * summed_first)
         + jnp.sum(summed_second * summed_second)

time: 396 us -> 187 us (0.47)
  waiting for transfers between devices: 178 us -> 1.48 us
  blocking collectives: 112 us -> 0 us
  Pallas kernels: 0 us -> 62.3 us
  matrix products: 25.2 us -> 54.2 us
  between operations: 16.9 us -> 3.75 us
  local copies, waits for them, and re-layouts: 2.73 us -> 8.18 us
    psum x1 -> x0, waiting for transfers between devices: 177 us -> none  [body(): lax.psum((raw_first, raw_second, raw_vectors), ('tm', 'row'))]
    psum x1 -> x0, blocking collectives: 112 us -> none  [body(): lax.psum((raw_first, raw_second, raw_vectors), ('tm', 'row'))]
    pallas_call x0 -> x1, Pallas kernels: none -> 62.3 us  [all_sum(): pl.pallas_call(reduce_kernel, out_shape=jax.ShapeDtypeStruct((ROWS_ALL, L...]
    dot_general x54, matrix products: 9.13 us -> 25.8 us  [kernel_grad(): jnp.einsum('otrw,ctrw->oc', upstream, window, preferred_element_type=jnp....]
    dot_general x54, matrix products: 11.7 us -> 24 us  [input_grad(): jnp.einsum('oc,otrw->ctrw', kernel[tap_t, tap_h, tap_w], window, preferre...]
    mul x0 -> x3, local copies, waits for them, and re-layouts: none -> 4.63 us  [the longest x1 2.56 us: body(): grad_kernel_first = summed_first * factor]
  transfers between devices with their start and end apart: 17 -> 16, of which waited for: 3 -> 1; matrix products, arithmetic and copies ran while one was open for 4% -> 11% of each run, Pallas kernels for 0% -> 0%
where the time goes in v1:
time: 187 us; the launch traced here: 186 us
  Pallas kernels  62.3 us (33%)
  matrix products  54.2 us (29%)
  starting transfers between devices  44.7 us (24%)
  other arithmetic  11.2 us (6%)
  local copies, waits for them, and re-layouts  8.18 us (4%)
  between operations  3.75 us (2%)
    pallas_call x1, Pallas kernels, all_sum(): pl.pallas_call(reduce_kernel, out_shape=jax.ShapeDtypeStruct((ROWS_ALL, L...  62.3 us
    dot_general x54, matrix products, kernel_grad(): jnp.einsum('otrw,ctrw->oc', upstream, window, preferred_element_type=jnp....  25.8 us
    ppermute x8, starting transfers between devices, shifted(): return lax.ppermute(block, axis, route)  25.3 us
    dot_general x54, matrix products, input_grad(): jnp.einsum('oc,otrw->ctrw', kernel[tap_t, tap_h, tap_w], window, preferre...  24 us
    ppermute x4, starting transfers between devices, extended(): lax.ppermute(lax.slice_in_dim(block, block.shape[dim] - width, None, axis...  14.1 us
    ppermute x4, starting transfers between devices, extended(): lax.ppermute(lax.slice_in_dim(block, 0, width, axis=dim), axis, backward)  5.34 us
    dot_general x27, matrix products, forward_conv(): jnp.einsum('oc,ctrw->otrw', kernel[tap_t, tap_h, tap_w], window, preferre...  4.39 us
  transfers between devices with their start and end apart: 16, of which 1 were waited for; matrix products, arithmetic and copies ran while one was open for 11% of the time, Pallas kernels for 0%

profile of v1, /device:TPU:1, one launch (start us, length us, event | category | flops | bytes accessed | tf_op | source)
XLA Modules:
  0.0 185.8 jit_solution(1084740042446511820)
XLA Ops:
  0.6 8.9 %collective-permute-start = (bf16[96,1,256]{2,0,1:T(8,128)(2,1)}, bf16[96,1,256]{2,0,1:T(8,128)(2,1)S(1)}, u32[]{:S(2)}, u32[]{:S(2)}) collective-permute-start(bf16[96,1,256]{2,0,1:T(8,128)(2,1)} %bitcast.1120), channel_id=1, source_target_pairs={{64,0},{128,64},{192,128},{256,192},{320,256},{384,320},{448,384},... | collective-permute-start | bytes 147464 | tf_op jit(solution)/shard_map/ppermute | solution.py:15
  9.6 1.3 collective-permute-start.1
  10.9 0.8 fusion.146
  11.7 0.9 fusion.394
  12.6 4.0 %collective-permute-start.4 = (bf16[96,1,256]{2,0,1:T(8,128)(2,1)S(1)}, bf16[96,1,256]{2,0,1:T(8,128)(2,1)S(1)}, u32[]{:S(2)}, u32[]{:S(2)}) collective-permute-start(bf16[96,1,256]{2,0,1:T(8,128)(2,1)S(1)} %fusion.394), channel_id=1, source_target_pairs={{0,128},{64,192},{128,256},{192,320},{256,384},{320,448},{1,129},{... | collective-permute-start | bytes 147464 | tf_op jit(solution)/shard_map/ppermute | solution.py:15
  16.6 1.9 %collective-permute-start.5 = (bf16[96,1,256]{2,0,1:T(8,128)(2,1)S(1)}, bf16[96,1,256]{2,0,1:T(8,128)(2,1)S(1)}, u32[]{:S(2)}, u32[]{:S(2)}) collective-permute-start(bf16[96,1,256]{2,0,1:T(8,128)(2,1)S(1)} %fusion.394), channel_id=1, source_target_pairs={{0,64},{64,128},{128,192},{192,256},{256,320},{320,384},{384,448},... | collective-permute-start | bytes 147464 | tf_op jit(solution)/shard_map/ppermute | solution.py:15
  18.6 0.8 pad_maximum_fusion
  19.4 1.3 collective-permute-start.2
  20.7 1.3 collective-permute-start.3
  22.0 0.9 fusion.139
  23.0 4.0 %collective-permute-start.6 = (bf16[96,3,1,256]{3,0,2,1:T(8,128)(2,1)S(1)}, bf16[96,3,1,256]{3,0,2,1:T(8,128)(2,1)S(1)}, u32[]{:S(2)}, u32[]{:S(2)}) collective-permute-start(bf16[96,3,1,256]{3,0,2,1:T(8,128)(2,1)S(1)} %pad_maximum_fusion.1), channel_id=1, source_target_pairs={{0,1},{1,2},{2,3},{3,4},{4,5},{5,6},{6,7},{7,8},{8,9},{9,10},{10,1... | collective-permute-start | bytes 442376 | tf_op jit(solution)/shard_map/ppermute | solution.py:23
  27.0 1.3 collective-permute-start.7
  28.3 1.1 fusion.122
  31.4 1.4 collective-permute-done.7
  42.0 1.9 %collective-permute-start.12 = (bf16[96,1,256]{2,0,1:T(8,128)(2,1)S(1)}, bf16[96,1,256]{2,0,1:T(8,128)(2,1)S(1)}, u32[]{:S(2)}, u32[]{:S(2)}) collective-permute-start(bf16[96,1,256]{2,0,1:T(8,128)(2,1)S(1)} %bitcast.1126), channel_id=1, source_target_pairs={{0,128},{64,192},{128,256},{192,320},{256,384},{320,448},{1,129},{... | collective-permute-start | bytes 147464 | tf_op jit(solution)/shard_map/ppermute | solution.py:15
  44.0 4.1 %collective-permute-start.13 = (bf16[96,1,256]{2,0,1:T(8,128)(2,1)S(1)}, bf16[96,1,256]{2,0,1:T(8,128)(2,1)S(1)}, u32[]{:S(2)}, u32[]{:S(2)}) collective-permute-start(bf16[96,1,256]{2,0,1:T(8,128)(2,1)S(1)} %bitcast.1127), channel_id=1, source_target_pairs={{0,64},{64,128},{128,192},{192,256},{256,320},{320,384},{384,448},... | collective-permute-start | bytes 147464 | tf_op jit(solution)/shard_map/ppermute | solution.py:15
  48.2 1.9 %collective-permute-start.8 = (bf16[96,1,256]{2,0,1:T(8,128)(2,1)S(1)}, bf16[96,1,256]{2,0,1:T(8,128)(2,1)S(1)}, u32[]{:S(2)}, u32[]{:S(2)}) collective-permute-start(bf16[96,1,256]{2,0,1:T(8,128)(2,1)S(1)} %bitcast.1122), channel_id=1, source_target_pairs={{64,0},{128,64},{192,128},{256,192},{320,256},{384,320},{448,384},... | collective-permute-start | bytes 147464 | tf_op jit(solution)/shard_map/ppermute | solution.py:15
  50.1 1.3 collective-permute-start.9
  56.5 4.0 %collective-permute-start.10 = (bf16[96,3,1,256]{3,0,2,1:T(8,128)(2,1)}, bf16[96,3,1,256]{3,0,2,1:T(8,128)(2,1)}, u32[]{:S(2)}, u32[]{:S(2)}) collective-permute-start(bf16[96,3,1,256]{3,0,2,1:T(8,128)(2,1)} %pad_maximum_fusion.2), channel_id=1, source_target_pairs={{0,1},{1,2},{2,3},{3,4},{4,5},{5,6},{6,7},{7,8},{8,9},{9,10},{10,1... | collective-permute-start | bytes 442376 | tf_op jit(solution)/shard_map/ppermute | solution.py:23
  60.4 1.3 collective-permute-start.11
  61.9 0.8 reshape_reshape.6
  62.8 4.8 %collective-permute-start.14 = (bf16[96,3,1,256]{3,0,2,1:T(8,128)(2,1)S(1)}, bf16[96,3,1,256]{3,0,2,1:T(8,128)(2,1)S(1)}, u32[]{:S(2)}, u32[]{:S(2)}) collective-permute-start(bf16[96,3,1,256]{3,0,2,1:T(8,128)(2,1)S(1)} %pad_maximum_fusion.3), channel_id=1, source_target_pairs={{0,1},{1,2},{2,3},{3,4},{4,5},{5,6},{6,7},{7,8},{8,9},{9,10},{10,1... | collective-permute-start | bytes 442376 | tf_op jit(solution)/shard_map/ppermute | solution.py:23
  67.6 1.5 collective-permute-start.15
  69.1 1.3 select_maximum_fusion.4
  70.4 0.9 fusion.152
  71.3 0.8 fusion.151
  72.1 0.9 fusion.150
  73.0 0.8 fusion.149
  73.8 0.8 fusion.148
  74.7 0.8 convolution_bitcast_fusion.19
  75.5 0.8 convolution_bitcast_fusion.16
  76.4 0.8 convolution_bitcast_fusion.10
  77.5 0.8 fusion.80
  78.3 0.8 fusion.79
  79.1 0.8 fusion.78
  80.7 0.8 fusion.76
  81.4 0.8 fusion.75
  83.0 0.8 fusion.73
  83.8 0.8 fusion.72
  85.4 0.8 fusion.70
  86.2 0.8 fusion.69
  87.7 0.8 fusion.67
  88.5 0.8 fusion.66
  90.1 0.8 fusion.64
  90.9 0.8 fusion.63
  93.2 0.8 fusion.60
  95.6 0.8 fusion.57
  97.9 0.8 fusion.54
  98.8 1.7 copy.11
  100.5 0.8 reshape_reshape.7
  101.4 1.3 convolution_add_fusion.23
  102.6 1.0 convolution_add_fusion.22
  103.6 1.1 convolution_add_fusion.21
  104.8 1.2 fusion.31
  105.9 1.1 convolution_add_fusion.19
  107.1 1.2 fusion.30
  109.5 1.0 fusion.27
  111.9 1.1 fusion.142
  113.1 0.8 convert_reduce_fusion
  114.2 62.3 %shard_map.102 = bf16[4096,128]{1,0:T(8,128)(2,1)S(1)} custom-call(f32[4096,128]{1,0:T(8,128)S(1)} %maximum_bitcast_fusion.z_ref), custom_call_target="tpu_custom_call" | custom-call | tf_op jit(solution)/shard_map/pallas_call | solution.py:239
  176.6 0.9 multiply_reduce_fusion
  180.1 1.1 slice_multiply_fusion
  181.8 2.6 %mul.245 = f32[3,3,3,96,96]{4,3,2,1,0:T(8,128)} reshape(f32[1944,128]{1,0:T(8,128)} %get-tuple-element.11) | data formatting | bytes 1990656 | tf_op jit(solution)/shard_map/mul | solution.py:312
  184.4 1.4 mul.247
  (170 shorter events, 29.1 us)
Async XLA Ops:
  0.6 28.8 %copy-start.6 = (bf16[3,3,3,96,96]{4,3,2,1,0:T(8,128)(2,1)S(1)}, bf16[3,3,3,96,96]{4,3,2,1,0:T(8,128)(2,1)}, u32[]{:S(2)}) copy-start(bf16[3,3,3,96,96]{4,3,2,1,0:T(8,128)(2,1)} %param.13) | copy-start | bytes 1492996
  0.6 17.9 %collective-permute-start = (bf16[96,1,256]{2,0,1:T(8,128)(2,1)}, bf16[96,1,256]{2,0,1:T(8,128)(2,1)S(1)}, u32[]{:S(2)}, u32[]{:S(2)}) collective-permute-start(bf16[96,1,256]{2,0,1:T(8,128)(2,1)} %bitcast.1120), channel_id=1, source_target_pairs={{64,0},{128,64},{192,128},{256,192},{320,256},{384,320},{448,384},... | collective-permute-start | bytes 147464 | tf_op jit(solution)/shard_map/ppermute | solution.py:15
  9.6 9.0 %collective-permute-start.1 = (bf16[96,1,256]{2,0,1:T(8,128)(2,1)}, bf16[96,1,256]{2,0,1:T(8,128)(2,1)S(1)}, u32[]{:S(2)}, u32[]{:S(2)}) collective-permute-start(bf16[96,1,256]{2,0,1:T(8,128)(2,1)} %bitcast.1121), channel_id=1, source_target_pairs={{128,0},{192,64},{256,128},{320,192},{384,256},{448,320},{129,1},{... | collective-permute-start | bytes 147464 | tf_op jit(solution)/shard_map/ppermute | solution.py:15
  12.6 10.3 %collective-permute-start.4 = (bf16[96,1,256]{2,0,1:T(8,128)(2,1)S(1)}, bf16[96,1,256]{2,0,1:T(8,128)(2,1)S(1)}, u32[]{:S(2)}, u32[]{:S(2)}) collective-permute-start(bf16[96,1,256]{2,0,1:T(8,128)(2,1)S(1)} %fusion.394), channel_id=1, source_target_pairs={{0,128},{64,192},{128,256},{192,320},{256,384},{320,448},{1,129},{... | collective-permute-start | bytes 147464 | tf_op jit(solution)/shard_map/ppermute | solution.py:15
  16.6 6.3 %collective-permute-start.5 = (bf16[96,1,256]{2,0,1:T(8,128)(2,1)S(1)}, bf16[96,1,256]{2,0,1:T(8,128)(2,1)S(1)}, u32[]{:S(2)}, u32[]{:S(2)}) collective-permute-start(bf16[96,1,256]{2,0,1:T(8,128)(2,1)S(1)} %fusion.394), channel_id=1, source_target_pairs={{0,64},{64,128},{128,192},{192,256},{256,320},{320,384},{384,448},... | collective-permute-start | bytes 147464 | tf_op jit(solution)/shard_map/ppermute | solution.py:15
  19.4 8.9 %collective-permute-start.2 = (bf16[96,3,1,256]{3,0,2,1:T(8,128)(2,1)S(1)}, bf16[96,3,1,256]{3,0,2,1:T(8,128)(2,1)S(1)}, u32[]{:S(2)}, u32[]{:S(2)}) collective-permute-start(bf16[96,3,1,256]{3,0,2,1:T(8,128)(2,1)S(1)} %pad_maximum_fusion), channel_id=1, source_target_pairs={{0,1},{1,2},{2,3},{3,4},{4,5},{5,6},{6,7},{7,8},{8,9},{9,10},{10,1... | collective-permute-start | bytes 442376 | tf_op jit(solution)/shard_map/ppermute | solution.py:23
  20.7 7.6 %collective-permute-start.3 = (bf16[96,3,1,256]{3,0,2,1:T(8,128)(2,1)S(1)}, bf16[96,3,1,256]{3,0,2,1:T(8,128)(2,1)S(1)}, u32[]{:S(2)}, u32[]{:S(2)}) collective-permute-start(bf16[96,3,1,256]{3,0,2,1:T(8,128)(2,1)S(1)} %pad_maximum_fusion), channel_id=1, source_target_pairs={{1,0},{2,1},{3,2},{4,3},{5,4},{6,5},{7,6},{8,7},{9,8},{10,9},{11,1... | collective-permute-start | bytes 442376 | tf_op jit(solution)/shard_map/ppermute | solution.py:26
  23.0 8.4 %collective-permute-start.6 = (bf16[96,3,1,256]{3,0,2,1:T(8,128)(2,1)S(1)}, bf16[96,3,1,256]{3,0,2,1:T(8,128)(2,1)S(1)}, u32[]{:S(2)}, u32[]{:S(2)}) collective-permute-start(bf16[96,3,1,256]{3,0,2,1:T(8,128)(2,1)S(1)} %pad_maximum_fusion.1), channel_id=1, source_target_pairs={{0,1},{1,2},{2,3},{3,4},{4,5},{5,6},{6,7},{7,8},{8,9},{9,10},{10,1... | collective-permute-start | bytes 442376 | tf_op jit(solution)/shard_map/ppermute | solution.py:23
  27.0 5.9 %collective-permute-start.7 = (bf16[96,3,1,256]{3,0,2,1:T(8,128)(2,1)S(1)}, bf16[96,3,1,256]{3,0,2,1:T(8,128)(2,1)S(1)}, u32[]{:S(2)}, u32[]{:S(2)}) collective-permute-start(bf16[96,3,1,256]{3,0,2,1:T(8,128)(2,1)S(1)} %pad_maximum_fusion.1), channel_id=1, source_target_pairs={{1,0},{2,1},{3,2},{4,3},{5,4},{6,5},{7,6},{8,7},{9,8},{10,9},{11,1... | collective-permute-start | bytes 442376 | tf_op jit(solution)/shard_map/ppermute | solution.py:26
  29.4 3.8 %copy-start.3 = (bf16[3,3,3,96,96]{4,3,2,1,0:T(8,128)(2,1)S(1)}, bf16[3,3,3,96,96]{4,3,2,1,0:T(8,128)(2,1)}, u32[]{:S(2)}) copy-start(bf16[3,3,3,96,96]{4,3,2,1,0:T(8,128)(2,1)} %param.12) | copy-start | bytes 1492996
  36.1 1.8 copy-start
  40.0 1.4 copy-start.15
  40.1 1.4 copy-start.16
  42.0 20.7 %collective-permute-start.12 = (bf16[96,1,256]{2,0,1:T(8,128)(2,1)S(1)}, bf16[96,1,256]{2,0,1:T(8,128)(2,1)S(1)}, u32[]{:S(2)}, u32[]{:S(2)}) collective-permute-start(bf16[96,1,256]{2,0,1:T(8,128)(2,1)S(1)} %bitcast.1126), channel_id=1, source_target_pairs={{0,128},{64,192},{128,256},{192,320},{256,384},{320,448},{1,129},{... | collective-permute-start | bytes 147464 | tf_op jit(solution)/shard_map/ppermute | solution.py:15
  44.0 18.8 %collective-permute-start.13 = (bf16[96,1,256]{2,0,1:T(8,128)(2,1)S(1)}, bf16[96,1,256]{2,0,1:T(8,128)(2,1)S(1)}, u32[]{:S(2)}, u32[]{:S(2)}) collective-permute-start(bf16[96,1,256]{2,0,1:T(8,128)(2,1)S(1)} %bitcast.1127), channel_id=1, source_target_pairs={{0,64},{64,128},{128,192},{192,256},{256,320},{320,384},{384,448},... | collective-permute-start | bytes 147464 | tf_op jit(solution)/shard_map/ppermute | solution.py:15
  48.2 7.6 %collective-permute-start.8 = (bf16[96,1,256]{2,0,1:T(8,128)(2,1)S(1)}, bf16[96,1,256]{2,0,1:T(8,128)(2,1)S(1)}, u32[]{:S(2)}, u32[]{:S(2)}) collective-permute-start(bf16[96,1,256]{2,0,1:T(8,128)(2,1)S(1)} %bitcast.1122), channel_id=1, source_target_pairs={{64,0},{128,64},{192,128},{256,192},{320,256},{384,320},{448,384},... | collective-permute-start | bytes 147464 | tf_op jit(solution)/shard_map/ppermute | solution.py:15
  50.1 5.7 %collective-permute-start.9 = (bf16[96,1,256]{2,0,1:T(8,128)(2,1)S(1)}, bf16[96,1,256]{2,0,1:T(8,128)(2,1)S(1)}, u32[]{:S(2)}, u32[]{:S(2)}) collective-permute-start(bf16[96,1,256]{2,0,1:T(8,128)(2,1)S(1)} %bitcast.1123), channel_id=1, source_target_pairs={{128,0},{192,64},{256,128},{320,192},{384,256},{448,320},{129,1},{... | collective-permute-start | bytes 147464 | tf_op jit(solution)/shard_map/ppermute | solution.py:15
  56.5 12.6 %collective-permute-start.10 = (bf16[96,3,1,256]{3,0,2,1:T(8,128)(2,1)}, bf16[96,3,1,256]{3,0,2,1:T(8,128)(2,1)}, u32[]{:S(2)}, u32[]{:S(2)}) collective-permute-start(bf16[96,3,1,256]{3,0,2,1:T(8,128)(2,1)} %pad_maximum_fusion.2), channel_id=1, source_target_pairs={{0,1},{1,2},{2,3},{3,4},{4,5},{5,6},{6,7},{7,8},{8,9},{9,10},{10,1... | collective-permute-start | bytes 442376 | tf_op jit(solution)/shard_map/ppermute | solution.py:23
  60.4 8.7 %collective-permute-start.11 = (bf16[96,3,1,256]{3,0,2,1:T(8,128)(2,1)}, bf16[96,3,1,256]{3,0,2,1:T(8,128)(2,1)S(1)}, u32[]{:S(2)}, u32[]{:S(2)}) collective-permute-start(bf16[96,3,1,256]{3,0,2,1:T(8,128)(2,1)} %pad_maximum_fusion.2), channel_id=1, source_target_pairs={{1,0},{2,1},{3,2},{4,3},{5,4},{6,5},{7,6},{8,7},{9,8},{10,9},{11,1... | collective-permute-start | bytes 442376 | tf_op jit(solution)/shard_map/ppermute | solution.py:26
  62.8 14.4 %collective-permute-start.14 = (bf16[96,3,1,256]{3,0,2,1:T(8,128)(2,1)S(1)}, bf16[96,3,1,256]{3,0,2,1:T(8,128)(2,1)S(1)}, u32[]{:S(2)}, u32[]{:S(2)}) collective-permute-start(bf16[96,3,1,256]{3,0,2,1:T(8,128)(2,1)S(1)} %pad_maximum_fusion.3), channel_id=1, source_target_pairs={{0,1},{1,2},{2,3},{3,4},{4,5},{5,6},{6,7},{7,8},{8,9},{9,10},{10,1... | collective-permute-start | bytes 442376 | tf_op jit(solution)/shard_map/ppermute | solution.py:23
  67.6 9.6 %collective-permute-start.15 = (bf16[96,3,1,256]{3,0,2,1:T(8,128)(2,1)S(1)}, bf16[96,3,1,256]{3,0,2,1:T(8,128)(2,1)S(1)}, u32[]{:S(2)}, u32[]{:S(2)}) collective-permute-start(bf16[96,3,1,256]{3,0,2,1:T(8,128)(2,1)S(1)} %pad_maximum_fusion.3), channel_id=1, source_target_pairs={{1,0},{2,1},{3,2},{4,3},{5,4},{6,5},{7,6},{8,7},{9,8},{10,9},{11,1... | collective-permute-start | bytes 442376 | tf_op jit(solution)/shard_map/ppermute | solution.py:26
  69.1 28.8 %copy-start.7 = (bf16[96,3,1,256]{3,0,2,1:T(8,128)(2,1)}, bf16[96,3,1,256]{3,0,2,1:T(8,128)(2,1)S(1)}, u32[]{:S(2)}) copy-start(bf16[96,3,1,256]{3,0,2,1:T(8,128)(2,1)S(1)} %collective-permute-done.11) | copy-start | bytes 442372
  70.4 6.8 %copy-start.1 = (bf16[96,3,3,258]{3,0,2,1:T(8,128)(2,1)}, bf16[96,3,3,258]{3,0,2,1:T(8,128)(2,1)S(1)}, u32[]{:S(2)}) copy-start(bf16[96,3,3,258]{3,0,2,1:T(8,128)(2,1)S(1)} %select_maximum_fusion.4) | copy-start | bytes 1337476
  101.3 5.8 %copy-start.4 = (bf16[3,3,3,96,96]{4,3,2,1,0:T(8,128)(2,1)S(1)}, bf16[3,3,3,96,96]{4,3,2,1,0:T(8,128)(2,1)}, u32[]{:S(2)}) copy-start(bf16[3,3,3,96,96]{4,3,2,1,0:T(8,128)(2,1)} %param.12) | copy-start | bytes 1492996
  101.3 6.9 %copy-start.2 = (bf16[96,3,3,258]{3,0,2,1:T(8,128)(2,1)S(1)}, bf16[96,3,3,258]{3,0,2,1:T(8,128)(2,1)}, u32[]{:S(2)}) copy-start(bf16[96,3,3,258]{3,0,2,1:T(8,128)(2,1)} %copy-done.1) | copy-start | bytes 1337476
  101.3 7.2 %copy-start.8 = (bf16[96,3,1,256]{3,0,2,1:T(8,128)(2,1)S(1)}, bf16[96,3,1,256]{3,0,2,1:T(8,128)(2,1)}, u32[]{:S(2)}) copy-start(bf16[96,3,1,256]{3,0,2,1:T(8,128)(2,1)} %copy-done.7) | copy-start | bytes 442372
  101.3 7.2 %copy-start.12 = (f32[256,96]{0,1:T(8,128)S(1)}, f32[256,96]{0,1:T(8,128)}, u32[]{:S(2)}) copy-start(f32[256,96]{0,1:T(8,128)} %fusion.149) | copy-start | bytes 294916
  101.4 7.6 %copy-start.11 = (f32[256,96]{0,1:T(8,128)S(1)}, f32[256,96]{0,1:T(8,128)}, u32[]{:S(2)}) copy-start(f32[256,96]{0,1:T(8,128)} %fusion.148) | copy-start | bytes 294916
  104.8 4.7 %copy-start.10 = (f32[96,256]{1,0:T(8,128)S(1)}, f32[96,256]{1,0:T(8,128)}, u32[]{:S(2)}) copy-start(f32[96,256]{1,0:T(8,128)} %convolution_bitcast_fusion.19) | copy-start | bytes 294916
  107.1 3.7 %copy-start.9 = (f32[96,256]{1,0:T(8,128)S(1)}, f32[96,256]{1,0:T(8,128)}, u32[]{:S(2)}) copy-start(f32[96,256]{1,0:T(8,128)} %convolution_bitcast_fusion.16) | copy-start | bytes 294916
  109.0 2.9 %copy-start.5 = (bf16[96,1,1,256]{3,0,2,1:T(8,128)(2,1)S(1)}, bf16[96,1,1,256]{3,0,2,1:T(8,128)(2,1)}, u32[]{:S(2)}) copy-start(bf16[96,1,1,256]{3,0,2,1:T(8,128)(2,1)} %param.7) | copy-start | bytes 147460
  109.0 2.9 %copy-start.13 = (f32[96,256]{1,0:T(8,128)S(1)}, f32[96,256]{1,0:T(8,128)}, u32[]{:S(2)}) copy-start(f32[96,256]{1,0:T(8,128)} %convolution_bitcast_fusion.10) | copy-start | bytes 294916
  109.0 2.9 %copy-start.14 = (f32[96]{0:T(128)S(1)}, f32[96]{0:T(128)}, u32[]{:S(2)}) copy-start(f32[96]{0:T(128)} %param.9) | copy-start | bytes 1156

commit v2 on v1

v2 whole, which is shorter than its diff:
```python
import jax
import jax.numpy as jnp
from jax import lax
from jax.experimental import pallas as pl
from jax.experimental.pallas import tpu as pltpu
from jax.sharding import PartitionSpec as P

epsilon = 1e-06
max_norm = 500.0
C = 96
W = 256
PACKED_ROWS = 4096
LANES = 128
VECTOR_ROW = 7 * 6 * C
MESH = pl.DeviceIdType.MESH
f32, bf16 = jnp.float32, jnp.bfloat16


def dot_nt(a, b):
    return lax.dot_general(a, b, (((1,), (1,)), ((), ())), preferred_element_type=f32)


def dot_nn(a, b):
    return lax.dot_general(a, b, (((1,), (0,)), ((), ())), preferred_element_type=f32)


def eye_mask():
    rows = lax.broadcasted_iota(jnp.int32, (C, C), 0)
    return rows == lax.broadcasted_iota(jnp.int32, (C, C), 1)


def to_column(row):
    spread = jnp.broadcast_to(row, (C, C))
    return jnp.sum(jnp.where(eye_mask(), spread, 0.0), axis=1, keepdims=True)


def to_row(column):
    spread = jnp.broadcast_to(column, (C, C))
    return jnp.sum(jnp.where(eye_mask(), spread, 0.0), axis=0, keepdims=True)


def shift_columns(values, offset):
    if offset == 0:
        return values
    column = lax.broadcasted_iota(jnp.int32, values.shape, 1)
    rolled = pltpu.roll(values, (-offset) % W, 1)
    edge = W - 1 if offset > 0 else 0
    return jnp.where(column == edge, 0.0, rolled)


def normalised(values):
    meansq = jnp.mean(values * values, axis=0, keepdims=True)
    inverse = lax.rsqrt(meansq + epsilon)
    return values * inverse, inverse


def act_parts(values, gain):
    unit, inverse = normalised(values)
    scaled = unit * gain
    gate = 1.0 / (1.0 + jnp.exp(-scaled))
    slope = gate * (1.0 + scaled * (1.0 - gate))
    return scaled * gate, slope, unit, inverse


def back_through_norm(grad_scaled, gain, unit, inverse):
    grad_unit = grad_scaled * gain
    return inverse * (grad_unit - unit * jnp.mean(grad_unit * unit, axis=0, keepdims=True))


CELLS = [(p, q) for p in range(3) for q in range(3)]
OWN = CELLS.index((2, 1))
ORDER = [7, 6, 8, 4, 1, 3, 5, 0, 2]


def band_of(cell):
    return pl.ds(cell * C, C)


def block_kernel(x_ref, cot_ref, gain_first_ref, gain_second_ref, bias_ref, k1_hbm, k2_hbm,
                 g_ref, grad_in_ref,
                 k1, k2, k1t, k2t, x_cells, c_cells, h_cells, f_cells, d_cells,
                 second3, hidden3, packed,
                 core_in, part, x_out, x_in, y_in, y_own, z_in, z_all,
                 local_sem, hx_sem, hc_sem, hh_sem,
                 core_sem, x_sem, y_sem, z_sem, gz_sem, gy_sem, gx_sem, gc_sem):
    tm, row = lax.axis_index("tm"), lax.axis_index("row")
    me_x, me_c = tm // 2, tm % 2
    me_z, me_y = row // 8, row % 8
    peer_c = {"tm": me_x * 2 + 1 - me_c, "row": row}

    def at_x(d):
        return lax.rem(me_x + d, 4)

    def at_y(d):
        return lax.rem(me_y + d, 8)

    def at_z(d):
        return lax.rem(me_z + d, 8)

    def peer_x(d):
        return {"tm": at_x(d) * 2 + me_c, "row": row}

    def peer_y(d):
        return {"tm": tm, "row": me_z * 8 + at_y(d)}

    def peer_z(d):
        return {"tm": tm, "row": at_z(d) * 8 + me_y}

    def later(cell):
        p, q = CELLS[cell]
        return {"tm": lax.rem(tm + 2 - p, 8), "row": lax.rem(row + 65 - q, 64)}

    def earlier(cell):
        p, q = CELLS[cell]
        return {"tm": lax.rem(tm + 6 + p, 8), "row": lax.rem(row + 63 + q, 64)}

    def send(src, dst, sems, slot, device):
        copy = pltpu.make_async_remote_copy(
            src_ref=src, dst_ref=dst, send_sem=sems.at[0, slot], recv_sem=sems.at[1, slot],
            device_id=device, device_id_type=MESH,
        )
        copy.start()
        return copy

    load_k1 = pltpu.make_async_copy(k1_hbm, k1, local_sem.at[0])
    load_k2 = pltpu.make_async_copy(k2_hbm, k2, local_sem.at[1])
    load_k1.start()
    load_k2.start()

    barrier = pltpu.get_barrier_semaphore()
    halo = [cell for cell in ORDER if cell != OWN]
    peers = [later(cell) for cell in halo] + [earlier(cell) for cell in halo]
    peers += [peer_c] + [peer_x(d) for d in range(1, 4)]
    peers += [peer_y(d) for d in range(1, 8)] + [peer_z(d) for d in range(1, 8)]
    for peer in peers:
        pl.semaphore_signal(barrier, inc=1, device_id=peer, device_id_type=MESH)
    pl.semaphore_wait(barrier, len(peers))

    sent = []
    x_copies, c_copies = {}, {}
    for cell in halo:
        x_copies[cell] = send(x_ref, x_cells.at[cell], hx_sem, cell, later(cell))
        c_copies[cell] = send(cot_ref, c_cells.at[band_of(cell)], hc_sem, cell, earlier(cell))
    sent += list(x_copies.values()) + list(c_copies.values())

    gain_first = to_column(gain_first_ref[...])
    gain_second = to_column(gain_second_ref[...])
    bias = to_column(bias_ref[...])
    identity = jnp.where(eye_mask(), 1.0, 0.0).astype(bf16)
    load_k1.wait()
    load_k2.wait()
    for cell in range(9):
        for s in range(3):
            band = pl.ds(s * C, C)
            k2t[cell, band, :] = dot_nt(identity, k2[cell, band, :]).astype(bf16)
            k1t[cell, band, :] = dot_nt(identity, k1[cell, band, :]).astype(bf16)

    pad = jnp.zeros((32, W), bf16)
    f_cells[pl.ds(9 * C, 32), :] = pad
    c_cells[pl.ds(9 * C, 32), :] = pad
    c_own = cot_ref[...]
    c_cells[band_of(OWN), :] = c_own

    def before(cell):
        p, q = CELLS[cell]
        return (tm + p >= 2) & (row + q >= 1) & (row + q <= 64)

    def after(cell):
        p, q = CELLS[cell]
        return (tm + 2 - p <= 7) & (row + 1 - q >= 0) & (row + 1 - q <= 63)

    sums = jnp.zeros((3 * C, W), f32)
    for cell in ORDER:
        if cell == OWN:
            wide = x_ref[...].astype(f32)
        else:
            x_copies[cell].wait_recv()

            @pl.when(jnp.logical_not(before(cell)))
            def _():
                x_cells[cell] = jnp.zeros((C, W), bf16)

            wide = x_cells[cell].astype(f32)
        value, slope, unit, inverse = act_parts(wide, gain_first)
        if cell == OWN:
            own_slope, own_unit, own_inverse = slope, unit, inverse
        band = band_of(cell)
        rounded = value.astype(bf16)
        f_cells[band, :] = rounded
        d_cells[band, :] = (slope * unit).astype(bf16)
        sums = sums + dot_nn(k1[cell], rounded)
    hidden = shift_columns(sums[:C], -1) + sums[C : 2 * C] + shift_columns(sums[2 * C :], 1)
    hidden = hidden + bias
    second, slope, unit, inverse = act_parts(hidden, gain_second)
    second = second.astype(bf16).astype(f32)
    for s in range(3):
        second3[pl.ds(s * C, C), :] = shift_columns(second, s - 1).astype(bf16)

    sums = jnp.zeros((3 * C, W), f32)
    for cell in ORDER:
        if cell != OWN:
            c_copies[cell].wait_recv()

            @pl.when(jnp.logical_not(after(cell)))
            def _():
                c_cells[band_of(cell), :] = jnp.zeros((C, W), bf16)

        sums = sums + dot_nn(k2t[cell], c_cells[band_of(cell), :])
    grad_second = shift_columns(sums[:C], 1) + sums[C : 2 * C] + shift_columns(sums[2 * C :], -1)
    grad_scaled = grad_second * slope
    raw_gain_second = jnp.sum(grad_scaled * unit, axis=1, keepdims=True)
    grad_hidden = back_through_norm(grad_scaled, gain_second, unit, inverse)
    raw_bias = jnp.sum(grad_hidden, axis=1, keepdims=True)
    rounded = grad_hidden.astype(bf16)
    raw_cot = jnp.sum(c_own.astype(f32), axis=1, keepdims=True)
    hidden_cot = rounded.astype(f32)
    for s in range(3):
        hidden3[pl.ds(s * C, C), :] = shift_columns(hidden_cot, 1 - s).astype(bf16)
    h_own = pl.ds(C, C)
    h_copies = {}
    for cell in halo:
        h_copies[cell] = send(hidden3.at[h_own], h_cells.at[cell], hh_sem, cell, earlier(cell))
    sent += list(h_copies.values())

    raw = dot_nt(second3[...], c_cells[...])
    for j in range(7):
        packed[pl.ds(j * 6 * C + 3 * C, 3 * C), :] = raw[:, j * LANES : (j + 1) * LANES]
    raw = dot_nt(hidden3[...], f_cells[...])
    for j in range(7):
        packed[pl.ds(j * 6 * C, 3 * C), :] = raw[:, j * LANES : (j + 1) * LANES]
    gained = jnp.zeros((3 * C, C), f32)
    for cell in range(9):
        gained = gained + k1[cell].astype(f32) * dot_nt(hidden3[...], d_cells[band_of(cell), :])
    packed[pl.ds(VECTOR_ROW, PACKED_ROWS - VECTOR_ROW), :] = jnp.zeros(
        (PACKED_ROWS - VECTOR_ROW, LANES), f32
    )
    packed[pl.ds(VECTOR_ROW, 1), pl.ds(0, C)] = to_row(raw_bias)
    packed[pl.ds(VECTOR_ROW + 1, 1), pl.ds(0, C)] = jnp.sum(gained, axis=0, keepdims=True)
    packed[pl.ds(VECTOR_ROW + 2, 1), pl.ds(0, C)] = to_row(raw_gain_second)
    packed[pl.ds(VECTOR_ROW + 3, 1), pl.ds(0, C)] = to_row(raw_cot)

    halves = []
    for k in range(4):
        chunk = at_x(k + 1) * 512
        theirs = pl.ds(pl.multiple_of((1 - me_c) * 2048 + chunk, 512), 512)
        land = pl.ds(pl.multiple_of(chunk, 512), 512)
        halves.append(send(packed.at[theirs], core_in.at[land], core_sem, k, peer_c))
    arrivals = []
    for k in range(4):
        halves[k].wait_recv()
        chunk = at_x(k + 1) * 512
        mine = pl.ds(pl.multiple_of(me_c * 2048 + chunk, 512), 512)
        land = pl.ds(pl.multiple_of(chunk, 512), 512)
        total = packed[mine, :] + core_in[land, :]
        if k < 3:
            x_out[k] = total.astype(jnp.bfloat16)
            arrivals.append(send(x_out.at[k], x_in.at[k], x_sem, k, peer_x(k + 1)))
        else:
            part[...] = total
    sent += halves + arrivals

    sums = dot_nn(k1t[OWN], hidden3[h_own, :])
    for cell in ORDER[1:]:
        h_copies[cell].wait_recv()

        @pl.when(jnp.logical_not(after(cell)))
        def _():
            h_cells[cell] = jnp.zeros((C, W), bf16)

        sums = sums + dot_nn(k1t[cell], h_cells[cell])
    grad_first = shift_columns(sums[:C], 1) + sums[C : 2 * C] + shift_columns(sums[2 * C :], -1)
    input_term = back_through_norm(grad_first * own_slope, gain_first, own_unit, own_inverse)
    grad_in_ref[...] = (c_own.astype(f32) + input_term).astype(bf16)

    for copy in arrivals:
        copy.wait_recv()
    total = part[...]
    for k in range(3):
        total = total + x_in[k].astype(jnp.float32)
    part[...] = total
    arrivals = []
    for d in range(1, 8):
        theirs = pl.ds(pl.multiple_of(at_y(d) * 64, 64), 64)
        arrivals.append(send(part.at[theirs], y_in.at[d - 1], y_sem, d - 1, peer_y(d)))
    sent += arrivals
    for copy in arrivals:
        copy.wait_recv()
    total = part[pl.ds(pl.multiple_of(me_y * 64, 64), 64), :]
    for k in range(7):
        total = total + y_in[k]
    y_own[...] = total
    arrivals = []
    for d in range(1, 8):
        theirs = pl.ds(pl.multiple_of(at_z(d) * 8, 8), 8)
        arrivals.append(send(y_own.at[theirs], z_in.at[d - 1], z_sem, d - 1, peer_z(d)))
    sent += arrivals
    for copy in arrivals:
        copy.wait_recv()
    own = pl.ds(pl.multiple_of(me_z * 8, 8), 8)
    total = y_own[own, :]
    for k in range(7):
        total = total + z_in[k]
    z_all[own, :] = total
    arrivals = []
    for d in range(1, 8):
        arrivals.append(send(z_all.at[own], z_all.at[own], gz_sem, d - 1, peer_z(d)))
    sent += arrivals
    for copy in arrivals:
        copy.wait_recv()
    base = me_c * 2048 + me_x * 512
    mine = pl.ds(pl.multiple_of(base + me_y * 64, 64), 64)
    g_ref[mine, :] = z_all[...].astype(jnp.bfloat16)
    arrivals = []
    for d in range(1, 8):
        arrivals.append(send(g_ref.at[mine], g_ref.at[mine], gy_sem, d - 1, peer_y(d)))
    sent += arrivals
    for copy in arrivals:
        copy.wait_recv()
    mine = pl.ds(pl.multiple_of(base, 512), 512)
    arrivals = []
    for d in range(1, 4):
        arrivals.append(send(g_ref.at[mine], g_ref.at[mine], gx_sem, d - 1, peer_x(d)))
    cores = [send(g_ref.at[mine], g_ref.at[mine], gc_sem, 0, peer_c)]
    sent += arrivals
    for d in range(1, 4):
        arrivals[d - 1].wait_recv()
        there = pl.ds(pl.multiple_of(me_c * 2048 + at_x(4 - d) * 512, 512), 512)
        cores.append(send(g_ref.at[there], g_ref.at[there], gc_sem, d, peer_c))
    sent += cores
    for copy in cores:
        copy.wait_recv()
    for copy in sent:
        copy.wait_send()


def scale_kernel(g_ref, first_ref, second_ref, vectors_ref):
    squares = jnp.zeros((512, LANES), f32)
    for k in range(8):
        part = g_ref[pl.ds(k * 512, 512), :].astype(f32)
        squares = squares + part * part
    squares = jnp.sum(jnp.sum(squares, axis=0, keepdims=True), axis=1, keepdims=True)
    total = jnp.sqrt(squares)
    factor = jnp.minimum(1.0, max_norm / (total + epsilon))
    target = lax.broadcasted_iota(jnp.int32, (C, LANES), 0)
    lane = lax.broadcasted_iota(jnp.int32, (C, LANES), 1)
    for cell in range(9):
        tiles = range(cell * C // LANES, (cell * C + C - 1) // LANES + 1)
        first = jnp.zeros((3 * C, C), f32)
        second = [jnp.zeros((C, C), f32) for _ in range(3)]
        for j in tiles:
            pick = jnp.where(lane + (j * LANES - cell * C) == target, 1.0, 0.0).astype(bf16)
            first = first + dot_nt(g_ref[pl.ds(j * 6 * C, 3 * C), :], pick)
            for s in range(3):
                start = j * 6 * C + 3 * C + s * C
                second[s] = second[s] + dot_nt(pick, g_ref[pl.ds(start, C), :])
        first_ref[cell] = first * factor
        for s in range(3):
            second_ref[cell, pl.ds(s * C, C), :] = second[s] * factor
    vectors = g_ref[pl.ds(VECTOR_ROW, 16), :].astype(f32)
    vectors_ref[...] = vectors[:4, :C] * factor


def body(inputs, cotangent, gain_first, gain_second, bias_first, kernel_first, kernel_second):
    dma, vmem = pltpu.SemaphoreType.DMA, pltpu.VMEM
    in_vmem = pl.BlockSpec(memory_space=pltpu.VMEM)
    in_any = pl.BlockSpec(memory_space=pl.ANY)
    summed, grad_inputs = pl.pallas_call(
        block_kernel,
        out_shape=(
            jax.ShapeDtypeStruct((PACKED_ROWS, LANES), bf16),
            jax.ShapeDtypeStruct((C, W), bf16),
        ),
        in_specs=[in_vmem] * 5 + [in_any] * 2,
        out_specs=(in_vmem, in_vmem),
        scratch_shapes=[
            vmem((9, 3 * C, C), bf16), vmem((9, 3 * C, C), bf16),
            vmem((9, 3 * C, C), bf16), vmem((9, 3 * C, C), bf16),
            vmem((9, C, W), bf16), vmem((9 * C + 32, W), bf16), vmem((9, C, W), bf16),
            vmem((9 * C + 32, W), bf16), vmem((9 * C, W), bf16),
            vmem((3 * C, W), bf16), vmem((3 * C, W), bf16),
            vmem((PACKED_ROWS, LANES), f32),
            vmem((2048, LANES), f32),
            vmem((512, LANES), f32),
            vmem((3, 512, LANES), bf16),
            vmem((3, 512, LANES), bf16),
            vmem((7, 64, LANES), f32),
            vmem((64, LANES), f32),
            vmem((7, 8, LANES), f32),
            vmem((64, LANES), f32),
            dma((2,)), dma((2, 9)), dma((2, 9)), dma((2, 9)),
            dma((2, 4)), dma((2, 3)), dma((2, 7)), dma((2, 7)),
            dma((2, 7)), dma((2, 7)), dma((2, 3)), dma((2, 4)),
        ],
        compiler_params=pltpu.CompilerParams(
            collective_id=0, has_side_effects=True, vmem_limit_bytes=48 * 1024 * 1024
        ),
    )(
        inputs.reshape(C, W), cotangent.reshape(C, W),
        gain_first.reshape(1, C), gain_second.reshape(1, C), bias_first.reshape(1, C),
        kernel_first.reshape(9, 3 * C, C), kernel_second.reshape(9, 3 * C, C),
    )
    grad_first, grad_second, vectors = pl.pallas_call(
        scale_kernel,
        out_shape=(
            jax.ShapeDtypeStruct((9, 3 * C, C), f32),
            jax.ShapeDtypeStruct((9, 3 * C, C), f32),
            jax.ShapeDtypeStruct((4, C), f32),
        ),
        in_specs=[in_vmem],
        out_specs=(in_vmem,) * 3,
        compiler_params=pltpu.CompilerParams(vmem_limit_bytes=32 * 1024 * 1024),
    )(summed)
    return (
        grad_inputs.reshape(inputs.shape),
        grad_first.reshape(kernel_first.shape),
        grad_second.reshape(kernel_second.shape),
        vectors,
    )


def solution(mesh):
    in_specs = (P(None, "tm", "row", None), P(None, "tm", "row", None), P(), P(), P(), P(), P())
    out_specs = (P(None, "tm", "row", None), P(), P(), P())
    return jax.shard_map(body, mesh=mesh, in_specs=in_specs, out_specs=out_specs, check_vma=False)
```

time: 187 us -> 83 us (0.44)
  matrix products: 54.2 us -> 0 us
  starting transfers between devices: 44.7 us -> 0 us
  Pallas kernels: 62.3 us -> 75.7 us
  other arithmetic: 11.2 us -> 0 us
  between operations: 3.75 us -> 0.66 us
    dot_general x135 -> x0, matrix products: 54.2 us -> none  [the longest x54 25.8 us: kernel_grad(): jnp.einsum('otrw,ctrw->oc', upstream, window, preferred_element_type=jnp....]
    ppermute x16 -> x0, starting transfers between devices: 44.7 us -> none  [the longest x8 25.3 us: shifted(): return lax.ppermute(block, axis, route)]
    pallas_call x1 -> x2, Pallas kernels: 62.3 us -> 75.7 us  [the longest x1 73 us: body(): pl.pallas_call(block_kernel, out_shape=(jax.ShapeDtypeStruct((PACKED_ROWS...]
    unnamed x34 -> x15, local copies, waits for them, and re-layouts: 0.09 us -> 6.35 us
    mul x3 -> x0, local copies, waits for them, and re-layouts: 4.63 us -> none  [the longest x1 2.56 us: body(): grad_kernel_first = summed_first * factor]
    another operation x3 -> x0, local copies, waits for them, and re-layouts: 3.36 us -> none  [the longest x1 1.73 us: kernel_grad(): stacked = jnp.stack(pieces)]
    reduce_sum x5 -> x0, other arithmetic: 3.31 us -> none  [the longest x1 0.86 us: body(): jnp.sum(summed_second * summed_second)]
    concatenate x4 -> x0, other arithmetic: 3.1 us -> none  [extended(): block = jnp.concatenate([low, block, high], axis=dim)]
  transfers between devices with their start and end apart: 16 -> 0, of which waited for: 1 -> 0; matrix products, arithmetic and copies ran while one was open for 11% -> 0% of each run, Pallas kernels for 0% -> 0%
where the time goes in v2:
time: 83 us; the launch traced here: 82.7 us
  Pallas kernels  75.7 us (91%)
  local copies, waits for them, and re-layouts  6.35 us (8%)
    pallas_call x1, Pallas kernels, body(): pl.pallas_call(block_kernel, out_shape=(jax.ShapeDtypeStruct((PACKED_ROWS...  73 us
    unnamed x15, local copies, waits for them, and re-layouts  6.35 us
    pallas_call x1, Pallas kernels, body(): pl.pallas_call(scale_kernel, out_shape=(jax.ShapeDtypeStruct((9, 3 * C, C...  2.65 us

profile of v2, /device:TPU:1, one launch (start us, length us, event | category | flops | bytes accessed | tf_op | source)
XLA Modules:
  0.0 82.7 jit_solution(628143117012849706)
XLA Ops:
  0.6 0.0 copy-start
  0.6 1.1 %copy-done = bf16[3,3,3,96,96]{4,3,2,1,0:T(8,128)(2,1)S(1)} copy-done((bf16[3,3,3,96,96]{4,3,2,1,0:T(8,128)(2,1)S(1)}, bf16[3,3,3,96,96]{4,3,2,1,0:T(8,128)(2,1)}, u32[]{:S(2)}) %copy-start) | copy-done | bytes 497688
  1.7 0.0 copy-start.1
  1.7 1.1 %copy-done.1 = bf16[3,3,3,96,96]{4,3,2,1,0:T(8,128)(2,1)S(1)} copy-done((bf16[3,3,3,96,96]{4,3,2,1,0:T(8,128)(2,1)S(1)}, bf16[3,3,3,96,96]{4,3,2,1,0:T(8,128)(2,1)}, u32[]{:S(2)}) %copy-start.1) | copy-done | bytes 497688
  2.8 0.0 copy-start.2
  2.8 0.8 copy-done.2
  3.6 0.0 copy-start.3
  3.6 0.8 copy-done.3
  4.4 0.0 copy-start.4
  4.4 0.7 copy-done.4
  5.1 0.0 copy-start.5
  5.1 0.7 copy-done.5
  5.7 0.0 copy-start.6
  5.7 0.7 copy-done.6
  6.4 73.0 %shard_map.102 = (bf16[4096,128]{1,0:T(8,128)(2,1)S(1)}, bf16[96,256]{1,0:T(8,128)(2,1)S(1)}) custom-call(bf16[96,256]{1,0:T(8,128)(2,1)S(1)} %bitcast.12, bf16[96,256]{1,0:T(8,128)(2,1)S(1)} %bitcast.13, f32[1,96]{1,0:T(1,128)S(1)} %bitcast.15, f32[1,96]{1,0:T(1,128)S(1)} %bitcast.16, f32[1,96]{1,0:T(1,128)S(1)} %bitcast.17, ...), custom_call_target="tpu_custom_call" | custom-call | tf_op jit(solution)/shard_map/pallas_call | solution.py:367
  79.4 2.7 %shard_map.103 = (f32[9,288,96]{2,1,0:T(8,128)}, f32[9,288,96]{2,1,0:T(8,128)}, f32[4,96]{1,0:T(4,128)}) custom-call(bf16[4096,128]{1,0:T(8,128)(2,1)S(1)} %get-tuple-element.10.g_ref), custom_call_target="tpu_custom_call" | custom-call | tf_op jit(solution)/shard_map/pallas_call | solution.py:402
  82.0 0.6 copy.12
Async XLA Ops:
  0.6 1.1 %copy-start = (bf16[3,3,3,96,96]{4,3,2,1,0:T(8,128)(2,1)S(1)}, bf16[3,3,3,96,96]{4,3,2,1,0:T(8,128)(2,1)}, u32[]{:S(2)}) copy-start(bf16[3,3,3,96,96]{4,3,2,1,0:T(8,128)(2,1)} %param.12) | copy-start | bytes 1492996
  1.7 1.1 %copy-start.1 = (bf16[3,3,3,96,96]{4,3,2,1,0:T(8,128)(2,1)S(1)}, bf16[3,3,3,96,96]{4,3,2,1,0:T(8,128)(2,1)}, u32[]{:S(2)}) copy-start(bf16[3,3,3,96,96]{4,3,2,1,0:T(8,128)(2,1)} %param.13) | copy-start | bytes 1492996
  2.8 0.8 copy-start.2
  3.6 0.8 copy-start.3
  4.4 0.7 copy-start.4
  5.1 0.7 copy-start.5
  5.7 0.7 copy-start.6

commit v3 on v2

--- a/solution.py
+++ b/solution.py
@@ -9,9 +9,9 @@
 max_norm = 500.0
 C = 96
 W = 256
-PACKED_ROWS = 4096
+HALF_ROWS = 2048
 LANES = 128
-VECTOR_ROW = 7 * 6 * C
+VECTOR_ROW = 7 * 3 * C
 MESH = pl.DeviceIdType.MESH
 f32, bf16 = jnp.float32, jnp.bfloat16
 
@@ -72,17 +72,30 @@
 ORDER = [7, 6, 8, 4, 1, 3, 5, 0, 2]
 
 
+FAR_FIRST = (4, 5, 3, 6, 2, 7, 1, 0)
+
+
 def band_of(cell):
     return pl.ds(cell * C, C)
 
 
-def block_kernel(x_ref, cot_ref, gain_first_ref, gain_second_ref, bias_ref, k1_hbm, k2_hbm,
+def put_rows(packed, half, raw):
+    for n in range(63):
+        start = n * 32
+        j, r = start // (3 * C), start % (3 * C)
+        block = start // 64
+        packed[half, block // 8, block % 8, pl.ds(start % 64, 32), :] = raw[
+            r : r + 32, j * LANES : (j + 1) * LANES
+        ]
+
+
+def block_kernel(x_hbm, cot_hbm, gain_first_hbm, gain_second_hbm, bias_hbm, k1_hbm, k2_hbm,
                  g_ref, grad_in_ref,
-                 k1, k2, k1t, k2t, x_cells, c_cells, h_cells, f_cells, d_cells,
+                 x_ref, cot_ref, gain_first_ref, gain_second_ref, bias_ref, k1, k2, k1t, k2t, x_cells, c_cells, h_cells, f_cells, d_cells,
                  second3, hidden3, packed,
-                 core_in, part, x_out, x_in, y_in, y_own, z_in, z_all,
+                 core_in, part, x_out, x_in, y_out, y_in, z_in,
                  local_sem, hx_sem, hc_sem, hh_sem,
-                 core_sem, x_sem, y_sem, z_sem, gz_sem, gy_sem, gx_sem, gc_sem):
+                 core_sem, x_sem, y_sem, z_sem, gy_sem, gx_sem, gc_sem):
     tm, row = lax.axis_index("tm"), lax.axis_index("row")
     me_x, me_c = tm // 2, tm % 2
     me_z, me_y = row // 8, row % 8
@@ -122,10 +135,11 @@
         copy.start()
         return copy
 
-    load_k1 = pltpu.make_async_copy(k1_hbm, k1, local_sem.at[0])
-    load_k2 = pltpu.make_async_copy(k2_hbm, k2, local_sem.at[1])
-    load_k1.start()
-    load_k2.start()
+    pairs = [(x_hbm, x_ref), (cot_hbm, cot_ref), (gain_first_hbm, gain_first_ref),
+             (gain_second_hbm, gain_second_ref), (bias_hbm, bias_ref), (k1_hbm, k1), (k2_hbm, k2)]
+    loads = [pltpu.make_async_copy(a, b, local_sem.at[k]) for k, (a, b) in enumerate(pairs)]
+    for load in loads:
+        load.start()
 
     barrier = pltpu.get_barrier_semaphore()
     halo = [cell for cell in ORDER if cell != OWN]
@@ -134,6 +148,8 @@
     peers += [peer_y(d) for d in range(1, 8)] + [peer_z(d) for d in range(1, 8)]
     for peer in peers:
         pl.semaphore_signal(barrier, inc=1, device_id=peer, device_id_type=MESH)
+    for load in loads[:2]:
+        load.wait()
     pl.semaphore_wait(barrier, len(peers))
 
     sent = []
@@ -143,12 +159,12 @@
         c_copies[cell] = send(cot_ref, c_cells.at[band_of(cell)], hc_sem, cell, earlier(cell))
     sent += list(x_copies.values()) + list(c_copies.values())
 
+    for load in loads[2:]:
+        load.wait()
     gain_first = to_column(gain_first_ref[...])
     gain_second = to_column(gain_second_ref[...])
     bias = to_column(bias_ref[...])
     identity = jnp.where(eye_mask(), 1.0, 0.0).astype(bf16)
-    load_k1.wait()
-    load_k2.wait()
     for cell in range(9):
         for s in range(3):
             band = pl.ds(s * C, C)
@@ -222,42 +238,33 @@
         h_copies[cell] = send(hidden3.at[h_own], h_cells.at[cell], hh_sem, cell, earlier(cell))
     sent += list(h_copies.values())
 
-    raw = dot_nt(second3[...], c_cells[...])
-    for j in range(7):
-        packed[pl.ds(j * 6 * C + 3 * C, 3 * C), :] = raw[:, j * LANES : (j + 1) * LANES]
-    raw = dot_nt(hidden3[...], f_cells[...])
-    for j in range(7):
-        packed[pl.ds(j * 6 * C, 3 * C), :] = raw[:, j * LANES : (j + 1) * LANES]
+    put_rows(packed, 1, dot_nt(second3[...], c_cells[...]))
+    put_rows(packed, 0, dot_nt(hidden3[...], f_cells[...]))
     gained = jnp.zeros((3 * C, C), f32)
     for cell in range(9):
         gained = gained + k1[cell].astype(f32) * dot_nt(hidden3[...], d_cells[band_of(cell), :])
-    packed[pl.ds(VECTOR_ROW, PACKED_ROWS - VECTOR_ROW), :] = jnp.zeros(
-        (PACKED_ROWS - VECTOR_ROW, LANES), f32
-    )
-    packed[pl.ds(VECTOR_ROW, 1), pl.ds(0, C)] = to_row(raw_bias)
-    packed[pl.ds(VECTOR_ROW + 1, 1), pl.ds(0, C)] = jnp.sum(gained, axis=0, keepdims=True)
-    packed[pl.ds(VECTOR_ROW + 2, 1), pl.ds(0, C)] = to_row(raw_gain_second)
-    packed[pl.ds(VECTOR_ROW + 3, 1), pl.ds(0, C)] = to_row(raw_cot)
-
-    halves = []
-    for k in range(4):
-        chunk = at_x(k + 1) * 512
-        theirs = pl.ds(pl.multiple_of((1 - me_c) * 2048 + chunk, 512), 512)
-        land = pl.ds(pl.multiple_of(chunk, 512), 512)
-        halves.append(send(packed.at[theirs], core_in.at[land], core_sem, k, peer_c))
-    arrivals = []
-    for k in range(4):
-        halves[k].wait_recv()
-        chunk = at_x(k + 1) * 512
-        mine = pl.ds(pl.multiple_of(me_c * 2048 + chunk, 512), 512)
-        land = pl.ds(pl.multiple_of(chunk, 512), 512)
-        total = packed[mine, :] + core_in[land, :]
-        if k < 3:
-            x_out[k] = total.astype(jnp.bfloat16)
-            arrivals.append(send(x_out.at[k], x_in.at[k], x_sem, k, peer_x(k + 1)))
-        else:
-            part[...] = total
-    sent += halves + arrivals
+    packed[0, 3, 7, pl.ds(32, 32), :] = jnp.zeros((32, LANES), f32)
+    packed[1, 3, 7, pl.ds(32, 32), :] = jnp.zeros((32, LANES), f32)
+    lanes = pl.ds(0, C)
+    packed[0, 3, 7, pl.ds(32, 1), lanes] = to_row(raw_bias)
+    packed[0, 3, 7, pl.ds(33, 1), lanes] = jnp.sum(gained, axis=0, keepdims=True)
+    packed[0, 3, 7, pl.ds(34, 1), lanes] = to_row(raw_gain_second)
+    packed[0, 3, 7, pl.ds(35, 1), lanes] = to_row(raw_cot)
+
+    core_copies = []
+    for k, d in enumerate(FAR_FIRST):
+        core_copies.append(send(packed.at[1 - me_c, :, at_y(d)], core_in.at[k], core_sem, k, peer_c))
+    x_copies = []
+    for k, d in enumerate(FAR_FIRST):
+        core_copies[k].wait_recv()
+        total = packed[me_c, :, at_y(d)] + core_in[k]
+        x_out[k] = total.astype(bf16)
+        part[k] = packed[me_c, me_x, at_y(d)] + core_in[k, me_x]
+        for e in (2, 1, 3):
+            x_copies.append(
+                send(x_out.at[k, at_x(e)], x_in.at[k, e - 1], x_sem, k * 3 + e - 1, peer_x(e))
+            )
+    sent += core_copies + x_copies
 
     sums = dot_nn(k1t[OWN], hidden3[h_own, :])
     for cell in ORDER[1:]:
@@ -272,68 +279,58 @@
     input_term = back_through_norm(grad_first * own_slope, gain_first, own_unit, own_inverse)
     grad_in_ref[...] = (c_own.astype(f32) + input_term).astype(bf16)
 
-    for copy in arrivals:
+    y_copies = []
+    for k, d in enumerate(FAR_FIRST):
+        total = part[k]
+        for copy in x_copies[3 * k : 3 * k + 3]:
+            copy.wait_recv()
+        for e in range(3):
+            total = total + x_in[k, e].astype(f32)
+        if d > 0:
+            y_out[k] = total.astype(bf16)
+            y_copies.append(send(y_out.at[k], y_in.at[d - 1], y_sem, d - 1, peer_y(d)))
+    for copy in y_copies:
         copy.wait_recv()
-    total = part[...]
-    for k in range(3):
-        total = total + x_in[k].astype(jnp.float32)
-    part[...] = total
-    arrivals = []
-    for d in range(1, 8):
-        theirs = pl.ds(pl.multiple_of(at_y(d) * 64, 64), 64)
-        arrivals.append(send(part.at[theirs], y_in.at[d - 1], y_sem, d - 1, peer_y(d)))
-    sent += arrivals
-    for copy in arrivals:
+    for e in range(7):
+        total = total + y_in[e].astype(f32)
+
+    z_in[me_z] = total.astype(bf16)
+    z_copies = []
+    for d in (4, 3, 5, 2, 6, 1, 7):
+        z_copies.append(send(z_in.at[me_z], z_in.at[me_z], z_sem, d - 1, peer_z(d)))
+    for copy in z_copies:
         copy.wait_recv()
-    total = part[pl.ds(pl.multiple_of(me_y * 64, 64), 64), :]
-    for k in range(7):
-        total = total + y_in[k]
-    y_own[...] = total
-    arrivals = []
-    for d in range(1, 8):
-        theirs = pl.ds(pl.multiple_of(at_z(d) * 8, 8), 8)
-        arrivals.append(send(y_own.at[theirs], z_in.at[d - 1], z_sem, d - 1, peer_z(d)))
-    sent += arrivals
-    for copy in arrivals:
-        copy.wait_recv()
-    own = pl.ds(pl.multiple_of(me_z * 8, 8), 8)
-    total = y_own[own, :]
-    for k in range(7):
-        total = total + z_in[k]
-    z_all[own, :] = total
-    arrivals = []
-    for d in range(1, 8):
-        arrivals.append(send(z_all.at[own], z_all.at[own], gz_sem, d - 1, peer_z(d)))
-    sent += arrivals
-    for copy in arrivals:
-        copy.wait_recv()
-    base = me_c * 2048 + me_x * 512
-    mine = pl.ds(pl.multiple_of(base + me_y * 64, 64), 64)
-    g_ref[mine, :] = z_all[...].astype(jnp.bfloat16)
-    arrivals = []
-    for d in range(1, 8):
-        arrivals.append(send(g_ref.at[mine], g_ref.at[mine], gy_sem, d - 1, peer_y(d)))
-    sent += arrivals
-    for copy in arrivals:
-        copy.wait_recv()
-    mine = pl.ds(pl.multiple_of(base, 512), 512)
-    arrivals = []
-    for d in range(1, 4):
-        arrivals.append(send(g_ref.at[mine], g_ref.at[mine], gx_sem, d - 1, peer_x(d)))
-    cores = [send(g_ref.at[mine], g_ref.at[mine], gc_sem, 0, peer_c)]
-    sent += arrivals
-    for d in range(1, 4):
-        arrivals[d - 1].wait_recv()
-        there = pl.ds(pl.multiple_of(me_c * 2048 + at_x(4 - d) * 512, 512), 512)
-        cores.append(send(g_ref.at[there], g_ref.at[there], gc_sem, d, peer_c))
-    sent += cores
-    for copy in cores:
+    total = z_in[0].astype(f32)
+    for e in range(1, 8):
+        total = total + z_in[e].astype(f32)
+    g_ref[me_c, me_x, me_y] = total.astype(bf16)
+    sent += y_copies + z_copies
+
+    own = g_ref.at[me_c, me_x, me_y]
+    gy_copies, gx_copies, gc_copies = {}, {}, []
+    for d in (4, 3, 5, 2, 6, 1, 7):
+        gy_copies[d] = send(own, own, gy_sem, d - 1, peer_y(d))
+    for k, d in enumerate((0, 1, 7, 2, 6, 3, 5, 4)):
+        piece = g_ref.at[me_c, me_x, at_y(8 - d)]
+        if d > 0:
+            gy_copies[d].wait_recv()
+        for e in (2, 1, 3):
+            gx_copies[k, e] = send(piece, piece, gx_sem, k * 3 + e - 1, peer_x(e))
+        gc_copies.append(send(piece, piece, gc_sem, k * 4, peer_c))
+    for k, d in enumerate((0, 1, 7, 2, 6, 3, 5, 4)):
+        for e in (1, 3, 2):
+            gx_copies[k, e].wait_recv()
+            piece = g_ref.at[me_c, at_x(4 - e), at_y(8 - d)]
+            gc_copies.append(send(piece, piece, gc_sem, k * 4 + e, peer_c))
+    sent += list(gy_copies.values()) + list(gx_copies.values()) + gc_copies
+    for copy in gc_copies:
         copy.wait_recv()
     for copy in sent:
         copy.wait_send()
 
 
-def scale_kernel(g_ref, first_ref, second_ref, vectors_ref):
+def scale_kernel(g_ref, grad_in_ref, first_ref, second_ref, vectors_ref, copy_ref):
+    copy_ref[...] = grad_in_ref[...]
     squares = jnp.zeros((512, LANES), f32)
     for k in range(8):
         part = g_ref[pl.ds(k * 512, 512), :].astype(f32)
@@ -349,9 +346,9 @@
         second = [jnp.zeros((C, C), f32) for _ in range(3)]
         for j in tiles:
             pick = jnp.where(lane + (j * LANES - cell * C) == target, 1.0, 0.0).astype(bf16)
-            first = first + dot_nt(g_ref[pl.ds(j * 6 * C, 3 * C), :], pick)
+            first = first + dot_nt(g_ref[pl.ds(j * 3 * C, 3 * C), :], pick)
             for s in range(3):
-                start = j * 6 * C + 3 * C + s * C
+                start = HALF_ROWS + j * 3 * C + s * C
                 second[s] = second[s] + dot_nt(pick, g_ref[pl.ds(start, C), :])
         first_ref[cell] = first * factor
         for s in range(3):
@@ -367,49 +364,51 @@
     summed, grad_inputs = pl.pallas_call(
         block_kernel,
         out_shape=(
-            jax.ShapeDtypeStruct((PACKED_ROWS, LANES), bf16),
+            jax.ShapeDtypeStruct((2, 4, 8, 64, LANES), bf16),
             jax.ShapeDtypeStruct((C, W), bf16),
         ),
-        in_specs=[in_vmem] * 5 + [in_any] * 2,
+        in_specs=[in_any] * 7,
         out_specs=(in_vmem, in_vmem),
         scratch_shapes=[
+            vmem((C, W), bf16), vmem((C, W), bf16),
+            vmem((1, C), f32), vmem((1, C), f32), vmem((1, C), f32),
             vmem((9, 3 * C, C), bf16), vmem((9, 3 * C, C), bf16),
             vmem((9, 3 * C, C), bf16), vmem((9, 3 * C, C), bf16),
             vmem((9, C, W), bf16), vmem((9 * C + 32, W), bf16), vmem((9, C, W), bf16),
             vmem((9 * C + 32, W), bf16), vmem((9 * C, W), bf16),
             vmem((3 * C, W), bf16), vmem((3 * C, W), bf16),
-            vmem((PACKED_ROWS, LANES), f32),
-            vmem((2048, LANES), f32),
-            vmem((512, LANES), f32),
-            vmem((3, 512, LANES), bf16),
-            vmem((3, 512, LANES), bf16),
-            vmem((7, 64, LANES), f32),
-            vmem((64, LANES), f32),
-            vmem((7, 8, LANES), f32),
-            vmem((64, LANES), f32),
-            dma((2,)), dma((2, 9)), dma((2, 9)), dma((2, 9)),
-            dma((2, 4)), dma((2, 3)), dma((2, 7)), dma((2, 7)),
-            dma((2, 7)), dma((2, 7)), dma((2, 3)), dma((2, 4)),
+            vmem((2, 4, 8, 64, LANES), f32),
+            vmem((8, 4, 64, LANES), f32),
+            vmem((8, 64, LANES), f32),
+            vmem((8, 4, 64, LANES), bf16),
+            vmem((8, 3, 64, LANES), bf16),
+            vmem((7, 64, LANES), bf16),
+            vmem((7, 64, LANES), bf16),
+            vmem((8, 64, LANES), bf16),
+            dma((7,)), dma((2, 9)), dma((2, 9)), dma((2, 9)),
+            dma((2, 8)), dma((2, 24)), dma((2, 7)), dma((2, 7)),
+            dma((2, 7)), dma((2, 24)), dma((2, 32)),
         ],
         compiler_params=pltpu.CompilerParams(
-            collective_id=0, has_side_effects=True, vmem_limit_bytes=48 * 1024 * 1024
+            collective_id=0, has_side_effects=True, vmem_limit_bytes=60 * 1024 * 1024
         ),
     )(
         inputs.reshape(C, W), cotangent.reshape(C, W),
         gain_first.reshape(1, C), gain_second.reshape(1, C), bias_first.reshape(1, C),
         kernel_first.reshape(9, 3 * C, C), kernel_second.reshape(9, 3 * C, C),
     )
-    grad_first, grad_second, vectors = pl.pallas_call(
+    grad_first, grad_second, vectors, grad_inputs = pl.pallas_call(
         scale_kernel,
         out_shape=(
             jax.ShapeDtypeStruct((9, 3 * C, C), f32),
             jax.ShapeDtypeStruct((9, 3 * C, C), f32),
             jax.ShapeDtypeStruct((4, C), f32),
+            jax.ShapeDtypeStruct((C, W), bf16),
         ),
-        in_specs=[in_vmem],
-        out_specs=(in_vmem,) * 3,
+        in_specs=[in_vmem] * 2,
+        out_specs=(in_vmem,) * 4,
         compiler_params=pltpu.CompilerParams(vmem_limit_bytes=32 * 1024 * 1024),
-    )(summed)
+    )(summed.reshape(2 * HALF_ROWS, LANES), grad_inputs)
     return (
         grad_inputs.reshape(inputs.shape),
         grad_first.reshape(kernel_first.shape),

time: 83 us -> 66.8 us (0.80)
  Pallas kernels: 75.7 us -> 63.9 us
  local copies, waits for them, and re-layouts: 6.35 us -> 2.02 us
    pallas_call x1, Pallas kernels: 73 us -> 61.3 us  [body(): pl.pallas_call(block_kernel, out_shape=(jax.ShapeDtypeStruct((2, 4, 8, 64...]
    unnamed x15 -> x4, local copies, waits for them, and re-layouts: 6.35 us -> 2.02 us
where the time goes in v3:
time: 66.8 us; the launch traced here: 66.6 us
  Pallas kernels  63.9 us (96%)
  local copies, waits for them, and re-layouts  2.02 us (3%)
    pallas_call x1, Pallas kernels, body(): pl.pallas_call(block_kernel, out_shape=(jax.ShapeDtypeStruct((2, 4, 8, 64...  61.3 us
    pallas_call x1, Pallas kernels, body(): pl.pallas_call(scale_kernel, out_shape=(jax.ShapeDtypeStruct((9, 3 * C, C...  2.65 us
    unnamed x4, local copies, waits for them, and re-layouts  2.02 us

profile of v3, /device:TPU:1, one launch (start us, length us, event | category | flops | bytes accessed | tf_op | source)
XLA Modules:
  0.0 66.6 jit_solution(17792914749403709363)
XLA Ops:
  0.6 61.3 %shard_map.102 = (bf16[2,4,8,64,128]{4,3,2,1,0:T(8,128)(2,1)}, bf16[96,256]{1,0:T(8,128)(2,1)}) custom-call(bf16[96,256]{1,0:T(8,128)(2,1)} %bitcast.14, bf16[96,256]{1,0:T(8,128)(2,1)} %bitcast.15, f32[1,96]{1,0:T(1,128)} %bitcast.16, f32[1,96]{1,0:T(1,128)} %bitcast.17, f32[1,96]{1,0:T(1,128)} %bitcast.18, bf16[9,288,96]{2,1,0:T(8,128)(2,1)} %bitcast.12, ...), custom_call_target="tpu_custom_call" | custom-call | tf_op jit(solution)/shard_map/pallas_call | solution.py:364
  61.9 0.0 copy-start
  61.9 1.2 %copy-done = bf16[2,4,8,64,128]{4,3,2,1,0:T(8,128)(2,1)S(1)} copy-done((bf16[2,4,8,64,128]{4,3,2,1,0:T(8,128)(2,1)S(1)}, bf16[2,4,8,64,128]{4,3,2,1,0:T(8,128)(2,1)}, u32[]{:S(2)}) %copy-start) | copy-done | bytes 1048600
  63.1 0.0 copy-start.1
  63.1 0.8 %copy-done.1 = bf16[96,256]{1,0:T(8,128)(2,1)S(1)} copy-done((bf16[96,256]{1,0:T(8,128)(2,1)S(1)}, bf16[96,256]{1,0:T(8,128)(2,1)}, u32[]{:S(2)}) %copy-start.1) | copy-done | bytes 49176
  63.9 2.6 %shard_map.103 = (f32[9,288,96]{2,1,0:T(8,128)}, f32[9,288,96]{2,1,0:T(8,128)}, f32[4,96]{1,0:T(4,128)}, bf16[96,256]{1,0:T(8,128)(2,1)}) custom-call(bf16[4096,128]{1,0:T(8,128)(2,1)S(1)} %bitcast.11, bf16[96,256]{1,0:T(8,128)(2,1)S(1)} %copy-done.1), custom_call_target="tpu_custom_call" | custom-call | tf_op jit(solution)/shard_map/pallas_call | solution.py:400
Async XLA Ops:
  61.9 1.2 %copy-start = (bf16[2,4,8,64,128]{4,3,2,1,0:T(8,128)(2,1)S(1)}, bf16[2,4,8,64,128]{4,3,2,1,0:T(8,128)(2,1)}, u32[]{:S(2)}) copy-start(bf16[2,4,8,64,128]{4,3,2,1,0:T(8,128)(2,1)} %get-tuple-element.10) | copy-start | bytes 3145732
  63.1 0.8 %copy-start.1 = (bf16[96,256]{1,0:T(8,128)(2,1)S(1)}, bf16[96,256]{1,0:T(8,128)(2,1)}, u32[]{:S(2)}) copy-start(bf16[96,256]{1,0:T(8,128)(2,1)} %get-tuple-element.11.grad_in_ref) | copy-start | bytes 147460

commit v4 on v3

--- a/solution.py
+++ b/solution.py
@@ -11,7 +11,6 @@
 W = 256
 HALF_ROWS = 2048
 LANES = 128
-VECTOR_ROW = 7 * 3 * C
 MESH = pl.DeviceIdType.MESH
 f32, bf16 = jnp.float32, jnp.bfloat16
 
@@ -90,12 +89,13 @@
 
 
 def block_kernel(x_hbm, cot_hbm, gain_first_hbm, gain_second_hbm, bias_hbm, k1_hbm, k2_hbm,
-                 g_ref, grad_in_ref,
-                 x_ref, cot_ref, gain_first_ref, gain_second_ref, bias_ref, k1, k2, k1t, k2t, x_cells, c_cells, h_cells, f_cells, d_cells,
+                 g_hbm, vector_ref, grad_in_ref,
+                 g_ref, x_ref, cot_ref, gain_first_ref, gain_second_ref, bias_ref, k1, k2, k1t, k2t, x_cells, c_cells, h_cells, f_cells, d_cells,
                  second3, hidden3, packed,
-                 core_in, part, x_out, x_in, y_out, y_in, z_in,
+                 core_in, part, x_out, x_in, y_out, y_in, z_in, vz, vy, vx, vc,
                  local_sem, hx_sem, hc_sem, hh_sem,
-                 core_sem, x_sem, y_sem, z_sem, gy_sem, gx_sem, gc_sem):
+                 core_sem, x_sem, y_sem, z_sem, gy_sem, gx_sem, gc_sem,
+                 vz_sem, vy_sem, vx_sem, vc_sem, out_sem):
     tm, row = lax.axis_index("tm"), lax.axis_index("row")
     me_x, me_c = tm // 2, tm % 2
     me_z, me_y = row // 8, row % 8
@@ -233,10 +233,6 @@
     for s in range(3):
         hidden3[pl.ds(s * C, C), :] = shift_columns(hidden_cot, 1 - s).astype(bf16)
     h_own = pl.ds(C, C)
-    h_copies = {}
-    for cell in halo:
-        h_copies[cell] = send(hidden3.at[h_own], h_cells.at[cell], hh_sem, cell, earlier(cell))
-    sent += list(h_copies.values())
 
     put_rows(packed, 1, dot_nt(second3[...], c_cells[...]))
     put_rows(packed, 0, dot_nt(hidden3[...], f_cells[...]))
@@ -245,11 +241,6 @@
         gained = gained + k1[cell].astype(f32) * dot_nt(hidden3[...], d_cells[band_of(cell), :])
     packed[0, 3, 7, pl.ds(32, 32), :] = jnp.zeros((32, LANES), f32)
     packed[1, 3, 7, pl.ds(32, 32), :] = jnp.zeros((32, LANES), f32)
-    lanes = pl.ds(0, C)
-    packed[0, 3, 7, pl.ds(32, 1), lanes] = to_row(raw_bias)
-    packed[0, 3, 7, pl.ds(33, 1), lanes] = jnp.sum(gained, axis=0, keepdims=True)
-    packed[0, 3, 7, pl.ds(34, 1), lanes] = to_row(raw_gain_second)
-    packed[0, 3, 7, pl.ds(35, 1), lanes] = to_row(raw_cot)
 
     core_copies = []
     for k, d in enumerate(FAR_FIRST):
@@ -266,18 +257,25 @@
             )
     sent += core_copies + x_copies
 
-    sums = dot_nn(k1t[OWN], hidden3[h_own, :])
-    for cell in ORDER[1:]:
-        h_copies[cell].wait_recv()
-
-        @pl.when(jnp.logical_not(after(cell)))
-        def _():
-            h_cells[cell] = jnp.zeros((C, W), bf16)
-
-        sums = sums + dot_nn(k1t[cell], h_cells[cell])
-    grad_first = shift_columns(sums[:C], 1) + sums[C : 2 * C] + shift_columns(sums[2 * C :], -1)
-    input_term = back_through_norm(grad_first * own_slope, gain_first, own_unit, own_inverse)
-    grad_in_ref[...] = (c_own.astype(f32) + input_term).astype(bf16)
+    vz[me_z] = jnp.zeros((8, LANES), f32)
+    lanes = pl.ds(0, C)
+    vz[me_z, pl.ds(0, 1), lanes] = to_row(raw_bias)
+    vz[me_z, pl.ds(1, 1), lanes] = jnp.sum(gained, axis=0, keepdims=True)
+    vz[me_z, pl.ds(2, 1), lanes] = to_row(raw_gain_second)
+    vz[me_z, pl.ds(3, 1), lanes] = to_row(raw_cot)
+    v_copies = [send(vz.at[me_z], vz.at[me_z], vz_sem, d - 1, peer_z(d)) for d in range(1, 8)]
+
+    def vector_total(slots, count):
+        for copy in v_copies:
+            copy.wait_recv()
+        sent.extend(v_copies)
+        whole = slots[0]
+        for e in range(1, count):
+            whole = whole + slots[e]
+        return whole
+
+    vy[me_y] = vector_total(vz, 8)
+    v_copies = [send(vy.at[me_y], vy.at[me_y], vy_sem, d - 1, peer_y(d)) for d in range(1, 8)]
 
     y_copies = []
     for k, d in enumerate(FAR_FIRST):
@@ -289,6 +287,10 @@
         if d > 0:
             y_out[k] = total.astype(bf16)
             y_copies.append(send(y_out.at[k], y_in.at[d - 1], y_sem, d - 1, peer_y(d)))
+    h_copies = {}
+    for cell in halo:
+        h_copies[cell] = send(hidden3.at[h_own], h_cells.at[cell], hh_sem, cell, earlier(cell))
+    sent += list(h_copies.values())
     for copy in y_copies:
         copy.wait_recv()
     for e in range(7):
@@ -298,6 +300,8 @@
     z_copies = []
     for d in (4, 3, 5, 2, 6, 1, 7):
         z_copies.append(send(z_in.at[me_z], z_in.at[me_z], z_sem, d - 1, peer_z(d)))
+    vx[me_x] = vector_total(vy, 8)
+    v_copies = [send(vx.at[me_x], vx.at[me_x], vx_sem, d - 1, peer_x(d)) for d in range(1, 4)]
     for copy in z_copies:
         copy.wait_recv()
     total = z_in[0].astype(f32)
@@ -310,36 +314,86 @@
     gy_copies, gx_copies, gc_copies = {}, {}, []
     for d in (4, 3, 5, 2, 6, 1, 7):
         gy_copies[d] = send(own, own, gy_sem, d - 1, peer_y(d))
-    for k, d in enumerate((0, 1, 7, 2, 6, 3, 5, 4)):
+
+    def pass_on(k, d):
         piece = g_ref.at[me_c, me_x, at_y(8 - d)]
-        if d > 0:
-            gy_copies[d].wait_recv()
         for e in (2, 1, 3):
             gx_copies[k, e] = send(piece, piece, gx_sem, k * 3 + e - 1, peer_x(e))
         gc_copies.append(send(piece, piece, gc_sem, k * 4, peer_c))
+
+    pass_on(0, 0)
+
+    sums = dot_nn(k1t[OWN], hidden3[h_own, :])
+    for cell in ORDER[1:]:
+        h_copies[cell].wait_recv()
+
+        @pl.when(jnp.logical_not(after(cell)))
+        def _():
+            h_cells[cell] = jnp.zeros((C, W), bf16)
+
+        sums = sums + dot_nn(k1t[cell], h_cells[cell])
+    grad_first = shift_columns(sums[:C], 1) + sums[C : 2 * C] + shift_columns(sums[2 * C :], -1)
+    input_term = back_through_norm(grad_first * own_slope, gain_first, own_unit, own_inverse)
+    grad_in_ref[...] = (c_own.astype(f32) + input_term).astype(bf16)
+
+    for k, d in enumerate((1, 7, 2, 6, 3, 5, 4)):
+        gy_copies[d].wait_recv()
+        pass_on(k + 1, d)
     for k, d in enumerate((0, 1, 7, 2, 6, 3, 5, 4)):
         for e in (1, 3, 2):
             gx_copies[k, e].wait_recv()
             piece = g_ref.at[me_c, at_x(4 - e), at_y(8 - d)]
             gc_copies.append(send(piece, piece, gc_sem, k * 4 + e, peer_c))
+        if k == 0:
+            vc[me_c] = vector_total(vx, 4)
+            v_copies = [send(vc.at[me_c], vc.at[me_c], vc_sem, 0, peer_c)]
+    outs = []
+
+    def store(c, x):
+        copy = pltpu.make_async_copy(g_ref.at[c, x], g_hbm.at[c, x], out_sem.at[len(outs)])
+        copy.start()
+        outs.append(copy)
+
+    for x in range(4):
+        store(me_c, x)
     sent += list(gy_copies.values()) + list(gx_copies.values()) + gc_copies
+    vector_ref[...] = vector_total(vc, 2)
     for copy in gc_copies:
         copy.wait_recv()
+    for x in range(4):
+        store(1 - me_c, x)
     for copy in sent:
         copy.wait_send()
-
-
-def scale_kernel(g_ref, grad_in_ref, first_ref, second_ref, vectors_ref, copy_ref):
-    copy_ref[...] = grad_in_ref[...]
-    squares = jnp.zeros((512, LANES), f32)
+    for copy in outs:
+        copy.wait()
+
+
+def scale_kernel(g_hbm, vector_hbm, grad_in_hbm, first_hbm, second_hbm, vectors_ref, copy_hbm,
+                 g_ref, vector_ref, first_ref, second_ref, load_sem, first_sem, second_sem):
+    through = pltpu.make_async_copy(grad_in_hbm, copy_hbm, load_sem.at[0])
+    vector_load = pltpu.make_async_copy(vector_hbm, vector_ref, load_sem.at[1])
+    loads = []
     for k in range(8):
-        part = g_ref[pl.ds(k * 512, 512), :].astype(f32)
-        squares = squares + part * part
-    squares = jnp.sum(jnp.sum(squares, axis=0, keepdims=True), axis=1, keepdims=True)
-    total = jnp.sqrt(squares)
+        rows = pl.ds(k * 512, 512)
+        loads.append(pltpu.make_async_copy(g_hbm.at[rows], g_ref.at[rows], load_sem.at[2 + k]))
+    for load in loads + [vector_load, through]:
+        load.start()
+    squares = jnp.zeros((64, LANES), f32)
+    for k in range(8):
+        loads[k].wait()
+        for n in range(8):
+            part = g_ref[pl.ds(k * 512 + n * 64, 64), :].astype(f32)
+            squares = squares + part * part
+    vector_load.wait()
+    vectors = vector_ref[...]
+    squares = jnp.sum(squares, axis=0, keepdims=True)
+    squares = squares + jnp.sum(vectors * vectors, axis=0, keepdims=True)
+    total = jnp.sqrt(jnp.sum(squares, axis=1, keepdims=True))
     factor = jnp.minimum(1.0, max_norm / (total + epsilon))
+    vectors_ref[...] = vectors[:4, :C] * factor
     target = lax.broadcasted_iota(jnp.int32, (C, LANES), 0)
     lane = lax.broadcasted_iota(jnp.int32, (C, LANES), 1)
+    stores = []
     for cell in range(9):
         tiles = range(cell * C // LANES, (cell * C + C - 1) // LANES + 1)
         first = jnp.zeros((3 * C, C), f32)
@@ -353,23 +407,34 @@
         first_ref[cell] = first * factor
         for s in range(3):
             second_ref[cell, pl.ds(s * C, C), :] = second[s] * factor
-    vectors = g_ref[pl.ds(VECTOR_ROW, 16), :].astype(f32)
-    vectors_ref[...] = vectors[:4, :C] * factor
+        stores.append(
+            pltpu.make_async_copy(first_ref.at[cell], first_hbm.at[cell], first_sem.at[cell])
+        )
+        stores[-1].start()
+        stores.append(
+            pltpu.make_async_copy(second_ref.at[cell], second_hbm.at[cell], second_sem.at[cell])
+        )
+        stores[-1].start()
+    through.wait()
+    for copy in stores:
+        copy.wait()
 
 
 def body(inputs, cotangent, gain_first, gain_second, bias_first, kernel_first, kernel_second):
     dma, vmem = pltpu.SemaphoreType.DMA, pltpu.VMEM
     in_vmem = pl.BlockSpec(memory_space=pltpu.VMEM)
     in_any = pl.BlockSpec(memory_space=pl.ANY)
-    summed, grad_inputs = pl.pallas_call(
+    summed, summed_vectors, grad_inputs = pl.pallas_call(
         block_kernel,
         out_shape=(
             jax.ShapeDtypeStruct((2, 4, 8, 64, LANES), bf16),
+            jax.ShapeDtypeStruct((8, LANES), f32),
             jax.ShapeDtypeStruct((C, W), bf16),
         ),
         in_specs=[in_any] * 7,
-        out_specs=(in_vmem, in_vmem),
+        out_specs=(in_any, in_vmem, in_vmem),
         scratch_shapes=[
+            vmem((2, 4, 8, 64, LANES), bf16),
             vmem((C, W), bf16), vmem((C, W), bf16),
             vmem((1, C), f32), vmem((1, C), f32), vmem((1, C), f32),
             vmem((9, 3 * C, C), bf16), vmem((9, 3 * C, C), bf16),
@@ -385,9 +450,12 @@
             vmem((7, 64, LANES), bf16),
             vmem((7, 64, LANES), bf16),
             vmem((8, 64, LANES), bf16),
+            vmem((8, 8, LANES), f32), vmem((8, 8, LANES), f32),
+            vmem((4, 8, LANES), f32), vmem((2, 8, LANES), f32),
             dma((7,)), dma((2, 9)), dma((2, 9)), dma((2, 9)),
             dma((2, 8)), dma((2, 24)), dma((2, 7)), dma((2, 7)),
             dma((2, 7)), dma((2, 24)), dma((2, 32)),
+            dma((2, 7)), dma((2, 7)), dma((2, 3)), dma((2, 1)), dma((8,)),
         ],
         compiler_params=pltpu.CompilerParams(
             collective_id=0, has_side_effects=True, vmem_limit_bytes=60 * 1024 * 1024
@@ -405,10 +473,15 @@
             jax.ShapeDtypeStruct((4, C), f32),
             jax.ShapeDtypeStruct((C, W), bf16),
         ),
-        in_specs=[in_vmem] * 2,
-        out_specs=(in_vmem,) * 4,
-        compiler_params=pltpu.CompilerParams(vmem_limit_bytes=32 * 1024 * 1024),
-    )(summed.reshape(2 * HALF_ROWS, LANES), grad_inputs)
+        in_specs=[in_any] * 3,
+        out_specs=(in_any, in_any, in_vmem, in_any),
+        scratch_shapes=[
+            vmem((2 * HALF_ROWS, LANES), bf16), vmem((8, LANES), f32),
+            vmem((9, 3 * C, C), f32), vmem((9, 3 * C, C), f32),
+            dma((10,)), dma((9,)), dma((9,)),
+        ],
+        compiler_params=pltpu.CompilerParams(vmem_limit_bytes=60 * 1024 * 1024),
+    )(summed.reshape(2 * HALF_ROWS, LANES), summed_vectors, grad_inputs)
     return (
         grad_inputs.reshape(inputs.shape),
         grad_first.reshape(kernel_first.shape),

time: 66.8 us -> 66.5 us (level)
  local copies, waits for them, and re-layouts: 2.02 us -> 0 us
  Pallas kernels: 63.9 us -> 65.7 us
    unnamed x4 -> x0, local copies, waits for them, and re-layouts: 2.02 us -> none
    pallas_call x1, Pallas kernels: 2.65 us -> 3.81 us  [body(): pl.pallas_call(scale_kernel, out_shape=(jax.ShapeDtypeStruct((9, 3 * C, C...]
where the time goes in v4:
time: 66.5 us; the launch traced here: 66.3 us
  Pallas kernels  65.7 us (99%)
    pallas_call x1, Pallas kernels, body(): pl.pallas_call(block_kernel, out_shape=(jax.ShapeDtypeStruct((2, 4, 8, 64...  61.9 us
    pallas_call x1, Pallas kernels, body(): pl.pallas_call(scale_kernel, out_shape=(jax.ShapeDtypeStruct((9, 3 * C, C...  3.81 us

profile of v4, /device:TPU:1, one launch (start us, length us, event | category | flops | bytes accessed | tf_op | source)
XLA Modules:
  0.0 66.3 jit_solution(2553409066505547393)
XLA Ops:
  0.6 61.9 %shard_map.102 = (bf16[2,4,8,64,128]{4,3,2,1,0:T(8,128)(2,1)}, f32[8,128]{1,0:T(8,128)}, bf16[96,256]{1,0:T(8,128)(2,1)}) custom-call(bf16[96,256]{1,0:T(8,128)(2,1)} %bitcast.14, bf16[96,256]{1,0:T(8,128)(2,1)} %bitcast.15, f32[1,96]{1,0:T(1,128)} %bitcast.16, f32[1,96]{1,0:T(1,128)} %bitcast.17, f32[1,96]{1,0:T(1,128)} %bitcast.18, ...), custom_call_target="tpu_custom_call" | custom-call | tf_op jit(solution)/shard_map/pallas_call | solution.py:427
  62.5 3.8 %shard_map.103 = (f32[9,288,96]{2,1,0:T(8,128)}, f32[9,288,96]{2,1,0:T(8,128)}, f32[4,96]{1,0:T(4,128)}, bf16[96,256]{1,0:T(8,128)(2,1)}) custom-call(bf16[4096,128]{1,0:T(8,128)(2,1)} %bitcast.11, f32[8,128]{1,0:T(8,128)} %get-tuple-element.12.vector_hbm, bf16[96,256]{1,0:T(8,128)(2,1)} %get-tuple-element.13.grad_in_hbm), custom_call_target="tpu_custom_call" | custom-call | tf_op jit(solution)/shard_map/pallas_call | solution.py:468

commit v5 on v4

--- a/solution.py
+++ b/solution.py
@@ -90,8 +90,8 @@
 
 def block_kernel(x_hbm, cot_hbm, gain_first_hbm, gain_second_hbm, bias_hbm, k1_hbm, k2_hbm,
                  g_hbm, vector_ref, grad_in_ref,
-                 g_ref, x_ref, cot_ref, gain_first_ref, gain_second_ref, bias_ref, k1, k2, k1t, k2t, x_cells, c_cells, h_cells, f_cells, d_cells,
-                 second3, hidden3, packed,
+                 g_ref, x_ref, cot_ref, gain_first_ref, gain_second_ref, bias_ref, k1, k2, k1t, k2t, x_cells, h_cells, d_cells,
+                 left, cells, packed,
                  core_in, part, x_out, x_in, y_out, y_in, z_in, vz, vy, vx, vc,
                  local_sem, hx_sem, hc_sem, hh_sem,
                  core_sem, x_sem, y_sem, z_sem, gy_sem, gx_sem, gc_sem,
@@ -156,7 +156,7 @@
     x_copies, c_copies = {}, {}
     for cell in halo:
         x_copies[cell] = send(x_ref, x_cells.at[cell], hx_sem, cell, later(cell))
-        c_copies[cell] = send(cot_ref, c_cells.at[band_of(cell)], hc_sem, cell, earlier(cell))
+        c_copies[cell] = send(cot_ref, cells.at[1, band_of(cell)], hc_sem, cell, earlier(cell))
     sent += list(x_copies.values()) + list(c_copies.values())
 
     for load in loads[2:]:
@@ -172,10 +172,10 @@
             k1t[cell, band, :] = dot_nt(identity, k1[cell, band, :]).astype(bf16)
 
     pad = jnp.zeros((32, W), bf16)
-    f_cells[pl.ds(9 * C, 32), :] = pad
-    c_cells[pl.ds(9 * C, 32), :] = pad
+    cells[0, pl.ds(9 * C, 32), :] = pad
+    cells[1, pl.ds(9 * C, 32), :] = pad
     c_own = cot_ref[...]
-    c_cells[band_of(OWN), :] = c_own
+    cells[1, band_of(OWN), :] = c_own
 
     def before(cell):
         p, q = CELLS[cell]
@@ -202,7 +202,7 @@
             own_slope, own_unit, own_inverse = slope, unit, inverse
         band = band_of(cell)
         rounded = value.astype(bf16)
-        f_cells[band, :] = rounded
+        cells[0, band, :] = rounded
         d_cells[band, :] = (slope * unit).astype(bf16)
         sums = sums + dot_nn(k1[cell], rounded)
     hidden = shift_columns(sums[:C], -1) + sums[C : 2 * C] + shift_columns(sums[2 * C :], 1)
@@ -210,7 +210,7 @@
     second, slope, unit, inverse = act_parts(hidden, gain_second)
     second = second.astype(bf16).astype(f32)
     for s in range(3):
-        second3[pl.ds(s * C, C), :] = shift_columns(second, s - 1).astype(bf16)
+        left[1, pl.ds(s * C, C), :] = shift_columns(second, s - 1).astype(bf16)
 
     sums = jnp.zeros((3 * C, W), f32)
     for cell in ORDER:
@@ -219,9 +219,9 @@
 
             @pl.when(jnp.logical_not(after(cell)))
             def _():
-                c_cells[band_of(cell), :] = jnp.zeros((C, W), bf16)
-
-        sums = sums + dot_nn(k2t[cell], c_cells[band_of(cell), :])
+                cells[1, band_of(cell), :] = jnp.zeros((C, W), bf16)
+
+        sums = sums + dot_nn(k2t[cell], cells[1, band_of(cell), :])
     grad_second = shift_columns(sums[:C], 1) + sums[C : 2 * C] + shift_columns(sums[2 * C :], -1)
     grad_scaled = grad_second * slope
     raw_gain_second = jnp.sum(grad_scaled * unit, axis=1, keepdims=True)
@@ -231,20 +231,16 @@
     raw_cot = jnp.sum(c_own.astype(f32), axis=1, keepdims=True)
     hidden_cot = rounded.astype(f32)
     for s in range(3):
-        hidden3[pl.ds(s * C, C), :] = shift_columns(hidden_cot, 1 - s).astype(bf16)
+        left[0, pl.ds(s * C, C), :] = shift_columns(hidden_cot, 1 - s).astype(bf16)
     h_own = pl.ds(C, C)
 
-    put_rows(packed, 1, dot_nt(second3[...], c_cells[...]))
-    put_rows(packed, 0, dot_nt(hidden3[...], f_cells[...]))
-    gained = jnp.zeros((3 * C, C), f32)
-    for cell in range(9):
-        gained = gained + k1[cell].astype(f32) * dot_nt(hidden3[...], d_cells[band_of(cell), :])
-    packed[0, 3, 7, pl.ds(32, 32), :] = jnp.zeros((32, LANES), f32)
-    packed[1, 3, 7, pl.ds(32, 32), :] = jnp.zeros((32, LANES), f32)
-
+    for half in (0, 1):
+        packed[half, 3, 7, pl.ds(32, 32), :] = jnp.zeros((32, LANES), f32)
+    put_rows(packed, 1 - me_c, dot_nt(left[1 - me_c], cells[1 - me_c]))
     core_copies = []
     for k, d in enumerate(FAR_FIRST):
         core_copies.append(send(packed.at[1 - me_c, :, at_y(d)], core_in.at[k], core_sem, k, peer_c))
+    put_rows(packed, me_c, dot_nt(left[me_c], cells[me_c]))
     x_copies = []
     for k, d in enumerate(FAR_FIRST):
         core_copies[k].wait_recv()
@@ -257,6 +253,9 @@
             )
     sent += core_copies + x_copies
 
+    gained = jnp.zeros((3 * C, C), f32)
+    for cell in range(9):
+        gained = gained + k1[cell].astype(f32) * dot_nt(left[0], d_cells[band_of(cell), :])
     vz[me_z] = jnp.zeros((8, LANES), f32)
     lanes = pl.ds(0, C)
     vz[me_z, pl.ds(0, 1), lanes] = to_row(raw_bias)
@@ -289,8 +288,7 @@
             y_copies.append(send(y_out.at[k], y_in.at[d - 1], y_sem, d - 1, peer_y(d)))
     h_copies = {}
     for cell in halo:
-        h_copies[cell] = send(hidden3.at[h_own], h_cells.at[cell], hh_sem, cell, earlier(cell))
-    sent += list(h_copies.values())
+        h_copies[cell] = send(left.at[0, h_own], h_cells.at[cell], hh_sem, cell, earlier(cell))
     for copy in y_copies:
         copy.wait_recv()
     for e in range(7):
@@ -300,6 +298,9 @@
     z_copies = []
     for d in (4, 3, 5, 2, 6, 1, 7):
         z_copies.append(send(z_in.at[me_z], z_in.at[me_z], z_sem, d - 1, peer_z(d)))
+    for copy in sent:
+        copy.wait_send()
+    sent = []
     vx[me_x] = vector_total(vy, 8)
     v_copies = [send(vx.at[me_x], vx.at[me_x], vx_sem, d - 1, peer_x(d)) for d in range(1, 4)]
     for copy in z_copies:
@@ -323,7 +324,10 @@
 
     pass_on(0, 0)
 
-    sums = dot_nn(k1t[OWN], hidden3[h_own, :])
+    for copy in sent:
+        copy.wait_send()
+    sent = list(h_copies.values())
+    sums = dot_nn(k1t[OWN], left[0, h_own, :])
     for cell in ORDER[1:]:
         h_copies[cell].wait_recv()
 
@@ -356,7 +360,9 @@
 
     for x in range(4):
         store(me_c, x)
-    sent += list(gy_copies.values()) + list(gx_copies.values()) + gc_copies
+    for copy in sent:
+        copy.wait_send()
+    sent = list(gy_copies.values()) + list(gx_copies.values()) + gc_copies
     vector_ref[...] = vector_total(vc, 2)
     for copy in gc_copies:
         copy.wait_recv()
@@ -439,9 +445,8 @@
             vmem((1, C), f32), vmem((1, C), f32), vmem((1, C), f32),
             vmem((9, 3 * C, C), bf16), vmem((9, 3 * C, C), bf16),
             vmem((9, 3 * C, C), bf16), vmem((9, 3 * C, C), bf16),
-            vmem((9, C, W), bf16), vmem((9 * C + 32, W), bf16), vmem((9, C, W), bf16),
-            vmem((9 * C + 32, W), bf16), vmem((9 * C, W), bf16),
-            vmem((3 * C, W), bf16), vmem((3 * C, W), bf16),
+            vmem((9, C, W), bf16), vmem((9, C, W), bf16), vmem((9 * C, W), bf16),
+            vmem((2, 3 * C, W), bf16), vmem((2, 9 * C + 32, W), bf16),
             vmem((2, 4, 8, 64, LANES), f32),
             vmem((8, 4, 64, LANES), f32),
             vmem((8, 64, LANES), f32),

time: 66.5 us -> 66.9 us (level)
  no operation moved by 1% of the time
where the time goes in v5:
time: 66.9 us; the launch traced here: 66.7 us
  Pallas kernels  66.1 us (99%)
    pallas_call x1, Pallas kernels, body(): pl.pallas_call(block_kernel, out_shape=(jax.ShapeDtypeStruct((2, 4, 8, 64...  62.3 us
    pallas_call x1, Pallas kernels, body(): pl.pallas_call(scale_kernel, out_shape=(jax.ShapeDtypeStruct((9, 3 * C, C...  3.81 us

profile of v5, /device:TPU:1, one launch (start us, length us, event | category | flops | bytes accessed | tf_op | source)
XLA Modules:
  0.0 66.7 jit_solution(5128357039851918519)
XLA Ops:
  0.6 62.3 %shard_map.102 = (bf16[2,4,8,64,128]{4,3,2,1,0:T(8,128)(2,1)}, f32[8,128]{1,0:T(8,128)}, bf16[96,256]{1,0:T(8,128)(2,1)}) custom-call(bf16[96,256]{1,0:T(8,128)(2,1)} %bitcast.14, bf16[96,256]{1,0:T(8,128)(2,1)} %bitcast.15, f32[1,96]{1,0:T(1,128)} %bitcast.16, f32[1,96]{1,0:T(1,128)} %bitcast.17, f32[1,96]{1,0:T(1,128)} %bitcast.18, ...), custom_call_target="tpu_custom_call" | custom-call | tf_op jit(solution)/shard_map/pallas_call | solution.py:433
  62.9 3.8 %shard_map.103 = (f32[9,288,96]{2,1,0:T(8,128)}, f32[9,288,96]{2,1,0:T(8,128)}, f32[4,96]{1,0:T(4,128)}, bf16[96,256]{1,0:T(8,128)(2,1)}) custom-call(bf16[4096,128]{1,0:T(8,128)(2,1)} %bitcast.11, f32[8,128]{1,0:T(8,128)} %get-tuple-element.12.vector_hbm, bf16[96,256]{1,0:T(8,128)(2,1)} %get-tuple-element.13.grad_in_hbm), custom_call_target="tpu_custom_call" | custom-call | tf_op jit(solution)/shard_map/pallas_call | solution.py:473

commit v6 on v5

--- a/solution.py
+++ b/solution.py
@@ -89,8 +89,8 @@
 
 
 def block_kernel(x_hbm, cot_hbm, gain_first_hbm, gain_second_hbm, bias_hbm, k1_hbm, k2_hbm,
-                 g_hbm, vector_ref, grad_in_ref,
-                 g_ref, x_ref, cot_ref, gain_first_ref, gain_second_ref, bias_ref, k1, k2, k1t, k2t, x_cells, h_cells, d_cells,
+                 g_hbm, stats_ref, grad_in_ref,
+                 g_ref, squares, x_ref, cot_ref, gain_first_ref, gain_second_ref, bias_ref, k1, k2, k1t, k2t, x_cells, h_cells, d_cells,
                  left, cells, packed,
                  core_in, part, x_out, x_in, y_out, y_in, z_in, vz, vy, vx, vc,
                  local_sem, hx_sem, hc_sem, hh_sem,
@@ -308,21 +308,37 @@
     total = z_in[0].astype(f32)
     for e in range(1, 8):
         total = total + z_in[e].astype(f32)
-    g_ref[me_c, me_x, me_y] = total.astype(bf16)
+    rounded = total.astype(bf16)
+    g_ref[me_c, me_x, me_y] = rounded
+    own_squares = rounded.astype(f32)
+    own_squares = own_squares * own_squares
     sent += y_copies + z_copies
 
     own = g_ref.at[me_c, me_x, me_y]
     gy_copies, gx_copies, gc_copies = {}, {}, []
     for d in (4, 3, 5, 2, 6, 1, 7):
         gy_copies[d] = send(own, own, gy_sem, d - 1, peer_y(d))
+
+    def square(c, x, y):
+        whole = jnp.zeros((16, LANES), f32)
+        for n in range(4):
+            part = g_ref[c, x, y, pl.ds(16 * n, 16), :].astype(f32)
+            whole = whole + part * part
+        squares[pl.ds(pl.multiple_of((c * 32 + x * 8 + y) * 16, 16), 16), :] = whole
 
     def pass_on(k, d):
         piece = g_ref.at[me_c, me_x, at_y(8 - d)]
         for e in (2, 1, 3):
             gx_copies[k, e] = send(piece, piece, gx_sem, k * 3 + e - 1, peer_x(e))
         gc_copies.append(send(piece, piece, gc_sem, k * 4, peer_c))
+        if d > 0:
+            square(me_c, me_x, at_y(8 - d))
 
     pass_on(0, 0)
+    own_rows = pl.ds(pl.multiple_of((me_c * 32 + me_x * 8 + me_y) * 16, 16), 16)
+    squares[own_rows, :] = (
+        own_squares[:16] + own_squares[16:32] + own_squares[32:48] + own_squares[48:]
+    )
 
     for copy in sent:
         copy.wait_send()
@@ -348,6 +364,7 @@
             gx_copies[k, e].wait_recv()
             piece = g_ref.at[me_c, at_x(4 - e), at_y(8 - d)]
             gc_copies.append(send(piece, piece, gc_sem, k * 4 + e, peer_c))
+            square(me_c, at_x(4 - e), at_y(8 - d))
         if k == 0:
             vc[me_c] = vector_total(vx, 4)
             v_copies = [send(vc.at[me_c], vc.at[me_c], vc_sem, 0, peer_c)]
@@ -363,43 +380,53 @@
     for copy in sent:
         copy.wait_send()
     sent = list(gy_copies.values()) + list(gx_copies.values()) + gc_copies
-    vector_ref[...] = vector_total(vc, 2)
-    for copy in gc_copies:
-        copy.wait_recv()
+    stats_ref[pl.ds(0, 8), :] = vector_total(vc, 2)
+    for k, d in enumerate((0, 1, 7, 2, 6, 3, 5, 4)):
+        gc_copies[k].wait_recv()
+        square(1 - me_c, me_x, at_y(8 - d))
+    for k, d in enumerate((0, 1, 7, 2, 6, 3, 5, 4)):
+        for n, e in enumerate((1, 3, 2)):
+            gc_copies[8 + 3 * k + n].wait_recv()
+            square(1 - me_c, at_x(4 - e), at_y(8 - d))
     for x in range(4):
         store(1 - me_c, x)
+
+    def add_squares(n, whole):
+        return whole + squares[pl.ds(pl.multiple_of(n * 128, 128), 128), :]
+
+    whole = lax.fori_loop(0, 8, add_squares, jnp.zeros((128, LANES), f32))
+    whole = jnp.sum(whole, axis=0, keepdims=True)
+    stats_ref[pl.ds(8, 8), :] = jnp.broadcast_to(whole * 0.125, (8, LANES))
     for copy in sent:
         copy.wait_send()
     for copy in outs:
         copy.wait()
 
 
-def scale_kernel(g_hbm, vector_hbm, grad_in_hbm, first_hbm, second_hbm, vectors_ref, copy_hbm,
-                 g_ref, vector_ref, first_ref, second_ref, load_sem, first_sem, second_sem):
+def scale_kernel(g_hbm, stats_hbm, grad_in_hbm, first_hbm, second_hbm, vectors_ref, copy_hbm,
+                 g_ref, stats_ref, first_ref, second_ref, load_sem, tile_sem, first_sem, second_sem):
     through = pltpu.make_async_copy(grad_in_hbm, copy_hbm, load_sem.at[0])
-    vector_load = pltpu.make_async_copy(vector_hbm, vector_ref, load_sem.at[1])
+    stats_load = pltpu.make_async_copy(stats_hbm, stats_ref, load_sem.at[1])
+    stats_load.start()
     loads = []
-    for k in range(8):
-        rows = pl.ds(k * 512, 512)
-        loads.append(pltpu.make_async_copy(g_hbm.at[rows], g_ref.at[rows], load_sem.at[2 + k]))
-    for load in loads + [vector_load, through]:
-        load.start()
-    squares = jnp.zeros((64, LANES), f32)
-    for k in range(8):
-        loads[k].wait()
-        for n in range(8):
-            part = g_ref[pl.ds(k * 512 + n * 64, 64), :].astype(f32)
-            squares = squares + part * part
-    vector_load.wait()
-    vectors = vector_ref[...]
-    squares = jnp.sum(squares, axis=0, keepdims=True)
-    squares = squares + jnp.sum(vectors * vectors, axis=0, keepdims=True)
-    total = jnp.sqrt(jnp.sum(squares, axis=1, keepdims=True))
+    for j in range(7):
+        for half in (0, 1):
+            rows = pl.ds(half * HALF_ROWS + j * 3 * C, 3 * C)
+            loads.append(pltpu.make_async_copy(g_hbm.at[rows], g_ref.at[rows], tile_sem.at[half, j]))
+            loads[-1].start()
+    through.start()
+    stats_load.wait()
+    stats = stats_ref[...]
+    kind = lax.broadcasted_iota(jnp.int32, (16, LANES), 0)
+    total = jnp.sum(jnp.where(kind < 8, stats * stats, stats), axis=1, keepdims=True)
+    total = jnp.sqrt(jnp.sum(total, axis=0, keepdims=True))
     factor = jnp.minimum(1.0, max_norm / (total + epsilon))
-    vectors_ref[...] = vectors[:4, :C] * factor
+    vectors_ref[...] = stats_ref[pl.ds(0, 4), pl.ds(0, C)] * factor
     target = lax.broadcasted_iota(jnp.int32, (C, LANES), 0)
     lane = lax.broadcasted_iota(jnp.int32, (C, LANES), 1)
     stores = []
+    for load in loads:
+        load.wait()
     for cell in range(9):
         tiles = range(cell * C // LANES, (cell * C + C - 1) // LANES + 1)
         first = jnp.zeros((3 * C, C), f32)
@@ -430,17 +457,17 @@
     dma, vmem = pltpu.SemaphoreType.DMA, pltpu.VMEM
     in_vmem = pl.BlockSpec(memory_space=pltpu.VMEM)
     in_any = pl.BlockSpec(memory_space=pl.ANY)
-    summed, summed_vectors, grad_inputs = pl.pallas_call(
+    summed, stats, grad_inputs = pl.pallas_call(
         block_kernel,
         out_shape=(
             jax.ShapeDtypeStruct((2, 4, 8, 64, LANES), bf16),
-            jax.ShapeDtypeStruct((8, LANES), f32),
+            jax.ShapeDtypeStruct((16, LANES), f32),
             jax.ShapeDtypeStruct((C, W), bf16),
         ),
         in_specs=[in_any] * 7,
         out_specs=(in_any, in_vmem, in_vmem),
         scratch_shapes=[
-            vmem((2, 4, 8, 64, LANES), bf16),
+            vmem((2, 4, 8, 64, LANES), bf16), vmem((1024, LANES), f32),
             vmem((C, W), bf16), vmem((C, W), bf16),
             vmem((1, C), f32), vmem((1, C), f32), vmem((1, C), f32),
             vmem((9, 3 * C, C), bf16), vmem((9, 3 * C, C), bf16),
@@ -481,12 +508,12 @@
         in_specs=[in_any] * 3,
         out_specs=(in_any, in_any, in_vmem, in_any),
         scratch_shapes=[
-            vmem((2 * HALF_ROWS, LANES), bf16), vmem((8, LANES), f32),
+            vmem((2 * HALF_ROWS, LANES), bf16), vmem((16, LANES), f32),
             vmem((9, 3 * C, C), f32), vmem((9, 3 * C, C), f32),
-            dma((10,)), dma((9,)), dma((9,)),
+            dma((2,)), dma((2, 7)), dma((9,)), dma((9,)),
         ],
         compiler_params=pltpu.CompilerParams(vmem_limit_bytes=60 * 1024 * 1024),
-    )(summed.reshape(2 * HALF_ROWS, LANES), summed_vectors, grad_inputs)
+    )(summed.reshape(2 * HALF_ROWS, LANES), stats, grad_inputs)
     return (
         grad_inputs.reshape(inputs.shape),
         grad_first.reshape(kernel_first.shape),

time: 66.9 us -> 67 us (level)
  no operation moved by 1% of the time
where the time goes in v6:
time: 67 us; the launch traced here: 66.8 us
  Pallas kernels  66.2 us (99%)
    pallas_call x1, Pallas kernels, body(): pl.pallas_call(block_kernel, out_shape=(jax.ShapeDtypeStruct((2, 4, 8, 64...  62.3 us
    pallas_call x1, Pallas kernels, body(): pl.pallas_call(scale_kernel, out_shape=(jax.ShapeDtypeStruct((9, 3 * C, C...  3.86 us

profile of v6, /device:TPU:1, one launch (start us, length us, event | category | flops | bytes accessed | tf_op | source)
XLA Modules:
  0.0 66.8 jit_solution(12616373548675006753)
XLA Ops:
  0.6 62.3 %shard_map.102 = (bf16[2,4,8,64,128]{4,3,2,1,0:T(8,128)(2,1)}, f32[16,128]{1,0:T(8,128)}, bf16[96,256]{1,0:T(8,128)(2,1)}) custom-call(bf16[96,256]{1,0:T(8,128)(2,1)} %bitcast.14, bf16[96,256]{1,0:T(8,128)(2,1)} %bitcast.15, f32[1,96]{1,0:T(1,128)} %bitcast.16, f32[1,96]{1,0:T(1,128)} %bitcast.17, f32[1,96]{1,0:T(1,128)} %bitcast.18, ...), custom_call_target="tpu_custom_call" | custom-call | tf_op jit(solution)/shard_map/pallas_call | solution.py:460
  63.0 3.9 %shard_map.103 = (f32[9,288,96]{2,1,0:T(8,128)}, f32[9,288,96]{2,1,0:T(8,128)}, f32[4,96]{1,0:T(4,128)}, bf16[96,256]{1,0:T(8,128)(2,1)}) custom-call(bf16[4096,128]{1,0:T(8,128)(2,1)} %bitcast.11, f32[16,128]{1,0:T(8,128)} %get-tuple-element.12.stats_hbm, bf16[96,256]{1,0:T(8,128)(2,1)} %get-tuple-element.13.grad_in_hbm), custom_call_target="tpu_custom_call" | custom-call | tf_op jit(solution)/shard_map/pallas_call | solution.py:500

commit v7 on v6

--- a/solution.py
+++ b/solution.py
@@ -89,13 +89,13 @@
 
 
 def block_kernel(x_hbm, cot_hbm, gain_first_hbm, gain_second_hbm, bias_hbm, k1_hbm, k2_hbm,
-                 g_hbm, stats_ref, grad_in_ref,
-                 g_ref, squares, x_ref, cot_ref, gain_first_ref, gain_second_ref, bias_ref, k1, k2, k1t, k2t, x_cells, h_cells, d_cells,
+                 g_ref, stats_ref, grad_in_ref,
+                 squares, x_ref, cot_ref, gain_first_ref, gain_second_ref, bias_ref, k1, k2, k1t, k2t, x_cells, h_cells, d_cells,
                  left, cells, packed,
                  core_in, part, x_out, x_in, y_out, y_in, z_in, vz, vy, vx, vc,
                  local_sem, hx_sem, hc_sem, hh_sem,
                  core_sem, x_sem, y_sem, z_sem, gy_sem, gx_sem, gc_sem,
-                 vz_sem, vy_sem, vx_sem, vc_sem, out_sem):
+                 vz_sem, vy_sem, vx_sem, vc_sem):
     tm, row = lax.axis_index("tm"), lax.axis_index("row")
     me_x, me_c = tm // 2, tm % 2
     me_z, me_y = row // 8, row % 8
@@ -368,15 +368,6 @@
         if k == 0:
             vc[me_c] = vector_total(vx, 4)
             v_copies = [send(vc.at[me_c], vc.at[me_c], vc_sem, 0, peer_c)]
-    outs = []
-
-    def store(c, x):
-        copy = pltpu.make_async_copy(g_ref.at[c, x], g_hbm.at[c, x], out_sem.at[len(outs)])
-        copy.start()
-        outs.append(copy)
-
-    for x in range(4):
-        store(me_c, x)
     for copy in sent:
         copy.wait_send()
     sent = list(gy_copies.values()) + list(gx_copies.values()) + gc_copies
@@ -388,8 +379,6 @@
         for n, e in enumerate((1, 3, 2)):
             gc_copies[8 + 3 * k + n].wait_recv()
             square(1 - me_c, at_x(4 - e), at_y(8 - d))
-    for x in range(4):
-        store(1 - me_c, x)
 
     def add_squares(n, whole):
         return whole + squares[pl.ds(pl.multiple_of(n * 128, 128), 128), :]
@@ -399,23 +388,12 @@
     stats_ref[pl.ds(8, 8), :] = jnp.broadcast_to(whole * 0.125, (8, LANES))
     for copy in sent:
         copy.wait_send()
-    for copy in outs:
-        copy.wait()
-
-
-def scale_kernel(g_hbm, stats_hbm, grad_in_hbm, first_hbm, second_hbm, vectors_ref, copy_hbm,
-                 g_ref, stats_ref, first_ref, second_ref, load_sem, tile_sem, first_sem, second_sem):
-    through = pltpu.make_async_copy(grad_in_hbm, copy_hbm, load_sem.at[0])
-    stats_load = pltpu.make_async_copy(stats_hbm, stats_ref, load_sem.at[1])
-    stats_load.start()
-    loads = []
-    for j in range(7):
-        for half in (0, 1):
-            rows = pl.ds(half * HALF_ROWS + j * 3 * C, 3 * C)
-            loads.append(pltpu.make_async_copy(g_hbm.at[rows], g_ref.at[rows], tile_sem.at[half, j]))
-            loads[-1].start()
+
+
+def scale_kernel(g_ref, stats_ref, grad_in_ref, first_hbm, second_hbm, vectors_ref, copy_hbm,
+                 first_ref, second_ref, copy_sem, first_sem, second_sem):
+    through = pltpu.make_async_copy(grad_in_ref, copy_hbm, copy_sem.at[0])
     through.start()
-    stats_load.wait()
     stats = stats_ref[...]
     kind = lax.broadcasted_iota(jnp.int32, (16, LANES), 0)
     total = jnp.sum(jnp.where(kind < 8, stats * stats, stats), axis=1, keepdims=True)
@@ -425,8 +403,6 @@
     target = lax.broadcasted_iota(jnp.int32, (C, LANES), 0)
     lane = lax.broadcasted_iota(jnp.int32, (C, LANES), 1)
     stores = []
-    for load in loads:
-        load.wait()
     for cell in range(9):
         tiles = range(cell * C // LANES, (cell * C + C - 1) // LANES + 1)
         first = jnp.zeros((3 * C, C), f32)
@@ -464,10 +440,10 @@
             jax.ShapeDtypeStruct((16, LANES), f32),
             jax.ShapeDtypeStruct((C, W), bf16),
         ),
-        in_specs=[in_any] * 7,
-        out_specs=(in_any, in_vmem, in_vmem),
+        in_specs=[pl.BlockSpec(memory_space=pltpu.HBM)] * 7,
+        out_specs=(in_vmem, in_vmem, in_vmem),
         scratch_shapes=[
-            vmem((2, 4, 8, 64, LANES), bf16), vmem((1024, LANES), f32),
+            vmem((1024, LANES), f32),
             vmem((C, W), bf16), vmem((C, W), bf16),
             vmem((1, C), f32), vmem((1, C), f32), vmem((1, C), f32),
             vmem((9, 3 * C, C), bf16), vmem((9, 3 * C, C), bf16),
@@ -487,15 +463,20 @@
             dma((7,)), dma((2, 9)), dma((2, 9)), dma((2, 9)),
             dma((2, 8)), dma((2, 24)), dma((2, 7)), dma((2, 7)),
             dma((2, 7)), dma((2, 24)), dma((2, 32)),
-            dma((2, 7)), dma((2, 7)), dma((2, 3)), dma((2, 1)), dma((8,)),
+            dma((2, 7)), dma((2, 7)), dma((2, 3)), dma((2, 1)),
         ],
         compiler_params=pltpu.CompilerParams(
-            collective_id=0, has_side_effects=True, vmem_limit_bytes=60 * 1024 * 1024
+            collective_id=0, has_side_effects=True, vmem_limit_bytes=44 * 1024 * 1024
         ),
     )(
-        inputs.reshape(C, W), cotangent.reshape(C, W),
-        gain_first.reshape(1, C), gain_second.reshape(1, C), bias_first.reshape(1, C),
-        kernel_first.reshape(9, 3 * C, C), kernel_second.reshape(9, 3 * C, C),
+        *(
+            pltpu.with_memory_space_constraint(operand, pltpu.HBM)
+            for operand in (
+                inputs.reshape(C, W), cotangent.reshape(C, W),
+                gain_first.reshape(1, C), gain_second.reshape(1, C), bias_first.reshape(1, C),
+                kernel_first.reshape(9, 3 * C, C), kernel_second.reshape(9, 3 * C, C),
+            )
+        )
     )
     grad_first, grad_second, vectors, grad_inputs = pl.pallas_call(
         scale_kernel,
@@ -505,14 +486,13 @@
             jax.ShapeDtypeStruct((4, C), f32),
             jax.ShapeDtypeStruct((C, W), bf16),
         ),
-        in_specs=[in_any] * 3,
+        in_specs=[in_vmem] * 3,
         out_specs=(in_any, in_any, in_vmem, in_any),
         scratch_shapes=[
-            vmem((2 * HALF_ROWS, LANES), bf16), vmem((16, LANES), f32),
             vmem((9, 3 * C, C), f32), vmem((9, 3 * C, C), f32),
-            dma((2,)), dma((2, 7)), dma((9,)), dma((9,)),
+            dma((1,)), dma((9,)), dma((9,)),
         ],
-        compiler_params=pltpu.CompilerParams(vmem_limit_bytes=60 * 1024 * 1024),
+        compiler_params=pltpu.CompilerParams(vmem_limit_bytes=44 * 1024 * 1024),
     )(summed.reshape(2 * HALF_ROWS, LANES), stats, grad_inputs)
     return (
         grad_inputs.reshape(inputs.shape),

time: 67 us -> 64.3 us (0.960)
  Pallas kernels: 66.2 us -> 63.5 us
    pallas_call x1, Pallas kernels: 3.86 us -> 2.44 us  [body(): pl.pallas_call(scale_kernel, out_shape=(jax.ShapeDtypeStruct((9, 3 * C, C...]
    pallas_call x1, Pallas kernels: 62.3 us -> 61 us  [body(): pl.pallas_call(block_kernel, out_shape=(jax.ShapeDtypeStruct((2, 4, 8, 64...]
where the time goes in v7:
time: 64.3 us; the launch traced here: 64.1 us
  Pallas kernels  63.5 us (99%)
    pallas_call x1, Pallas kernels, body(): pl.pallas_call(block_kernel, out_shape=(jax.ShapeDtypeStruct((2, 4, 8, 64...  61 us
    pallas_call x1, Pallas kernels, body(): pl.pallas_call(scale_kernel, out_shape=(jax.ShapeDtypeStruct((9, 3 * C, C...  2.44 us

profile of v7, /device:TPU:1, one launch (start us, length us, event | category | flops | bytes accessed | tf_op | source)
XLA Modules:
  0.0 64.1 jit_solution(15740739146063583553)
XLA Ops:
  0.6 61.0 %shard_map.102 = (bf16[2,4,8,64,128]{4,3,2,1,0:T(8,128)(2,1)S(1)}, f32[16,128]{1,0:T(8,128)S(1)}, bf16[96,256]{1,0:T(8,128)(2,1)S(1)}) custom-call(bf16[96,256]{1,0:T(8,128)(2,1)} %bitcast.14, bf16[96,256]{1,0:T(8,128)(2,1)} %bitcast.15, f32[1,96]{1,0:T(1,128)} %bitcast.16, f32[1,96]{1,0:T(1,128)} %bitcast.17, f32[1,96]{1,0:T(1,128)} %bitcast.18, ...), custom_call_target="tpu_custom_call" | custom-call | tf_op jit(solution)/shard_map/pallas_call | solution.py:436
  61.7 2.4 %shard_map.103 = (f32[9,288,96]{2,1,0:T(8,128)}, f32[9,288,96]{2,1,0:T(8,128)}, f32[4,96]{1,0:T(4,128)}, bf16[96,256]{1,0:T(8,128)(2,1)}) custom-call(bf16[4096,128]{1,0:T(8,128)(2,1)S(1)} %bitcast.11, f32[16,128]{1,0:T(8,128)S(1)} %get-tuple-element.12.stats_ref, bf16[96,256]{1,0:T(8,128)(2,1)S(1)} %get-tuple-element.13.grad_in_ref), custom_call_target="tpu_custom_call" | custom-call | tf_op jit(solution)/shard_map/pallas_call | solution.py:481

commit v8 on v7

--- a/solution.py
+++ b/solution.py
@@ -253,6 +253,10 @@
             )
     sent += core_copies + x_copies
 
+    h_copies = {}
+    for cell in halo:
+        h_copies[cell] = send(left.at[0, h_own], h_cells.at[cell], hh_sem, cell, earlier(cell))
+
     gained = jnp.zeros((3 * C, C), f32)
     for cell in range(9):
         gained = gained + k1[cell].astype(f32) * dot_nt(left[0], d_cells[band_of(cell), :])
@@ -273,9 +277,6 @@
             whole = whole + slots[e]
         return whole
 
-    vy[me_y] = vector_total(vz, 8)
-    v_copies = [send(vy.at[me_y], vy.at[me_y], vy_sem, d - 1, peer_y(d)) for d in range(1, 8)]
-
     y_copies = []
     for k, d in enumerate(FAR_FIRST):
         total = part[k]
@@ -286,9 +287,8 @@
         if d > 0:
             y_out[k] = total.astype(bf16)
             y_copies.append(send(y_out.at[k], y_in.at[d - 1], y_sem, d - 1, peer_y(d)))
-    h_copies = {}
-    for cell in halo:
-        h_copies[cell] = send(left.at[0, h_own], h_cells.at[cell], hh_sem, cell, earlier(cell))
+    vy[me_y] = vector_total(vz, 8)
+    v_copies = [send(vy.at[me_y], vy.at[me_y], vy_sem, d - 1, peer_y(d)) for d in range(1, 8)]
     for copy in y_copies:
         copy.wait_recv()
     for e in range(7):
@@ -301,6 +301,20 @@
     for copy in sent:
         copy.wait_send()
     sent = []
+    sums = dot_nn(k1t[OWN], left[0, h_own, :])
+    for cell in ORDER[1:]:
+        h_copies[cell].wait_recv()
+
+        @pl.when(jnp.logical_not(after(cell)))
+        def _():
+            h_cells[cell] = jnp.zeros((C, W), bf16)
+
+        sums = sums + dot_nn(k1t[cell], h_cells[cell])
+    grad_first = shift_columns(sums[:C], 1) + sums[C : 2 * C] + shift_columns(sums[2 * C :], -1)
+    input_term = back_through_norm(grad_first * own_slope, gain_first, own_unit, own_inverse)
+    grad_in_ref[...] = (c_own.astype(f32) + input_term).astype(bf16)
+
+    sent += list(h_copies.values())
     vx[me_x] = vector_total(vy, 8)
     v_copies = [send(vx.at[me_x], vx.at[me_x], vx_sem, d - 1, peer_x(d)) for d in range(1, 4)]
     for copy in z_copies:
@@ -339,22 +353,6 @@
     squares[own_rows, :] = (
         own_squares[:16] + own_squares[16:32] + own_squares[32:48] + own_squares[48:]
     )
-
-    for copy in sent:
-        copy.wait_send()
-    sent = list(h_copies.values())
-    sums = dot_nn(k1t[OWN], left[0, h_own, :])
-    for cell in ORDER[1:]:
-        h_copies[cell].wait_recv()
-
-        @pl.when(jnp.logical_not(after(cell)))
-        def _():
-            h_cells[cell] = jnp.zeros((C, W), bf16)
-
-        sums = sums + dot_nn(k1t[cell], h_cells[cell])
-    grad_first = shift_columns(sums[:C], 1) + sums[C : 2 * C] + shift_columns(sums[2 * C :], -1)
-    input_term = back_through_norm(grad_first * own_slope, gain_first, own_unit, own_inverse)
-    grad_in_ref[...] = (c_own.astype(f32) + input_term).astype(bf16)
 
     for k, d in enumerate((1, 7, 2, 6, 3, 5, 4)):
         gy_copies[d].wait_recv()

time: 64.3 us -> 64.4 us (level)
  no operation moved by 1% of the time
where the time goes in v8:
time: 64.4 us; the launch traced here: 64.3 us
  Pallas kernels  63.6 us (99%)
    pallas_call x1, Pallas kernels, body(): pl.pallas_call(block_kernel, out_shape=(jax.ShapeDtypeStruct((2, 4, 8, 64...  61.2 us
    pallas_call x1, Pallas kernels, body(): pl.pallas_call(scale_kernel, out_shape=(jax.ShapeDtypeStruct((9, 3 * C, C...  2.44 us

profile of v8, /device:TPU:1, one launch (start us, length us, event | category | flops | bytes accessed | tf_op | source)
XLA Modules:
  0.0 64.3 jit_solution(12134922433717443328)
XLA Ops:
  0.6 61.2 %shard_map.102 = (bf16[2,4,8,64,128]{4,3,2,1,0:T(8,128)(2,1)S(1)}, f32[16,128]{1,0:T(8,128)S(1)}, bf16[96,256]{1,0:T(8,128)(2,1)S(1)}) custom-call(bf16[96,256]{1,0:T(8,128)(2,1)} %bitcast.14, bf16[96,256]{1,0:T(8,128)(2,1)} %bitcast.15, f32[1,96]{1,0:T(1,128)} %bitcast.16, f32[1,96]{1,0:T(1,128)} %bitcast.17, f32[1,96]{1,0:T(1,128)} %bitcast.18, ...), custom_call_target="tpu_custom_call" | custom-call | tf_op jit(solution)/shard_map/pallas_call | solution.py:434
  61.8 2.4 %shard_map.103 = (f32[9,288,96]{2,1,0:T(8,128)}, f32[9,288,96]{2,1,0:T(8,128)}, f32[4,96]{1,0:T(4,128)}, bf16[96,256]{1,0:T(8,128)(2,1)}) custom-call(bf16[4096,128]{1,0:T(8,128)(2,1)S(1)} %bitcast.11, f32[16,128]{1,0:T(8,128)S(1)} %get-tuple-element.12.stats_ref, bf16[96,256]{1,0:T(8,128)(2,1)S(1)} %get-tuple-element.13.grad_in_ref), custom_call_target="tpu_custom_call" | custom-call | tf_op jit(solution)/shard_map/pallas_call | solution.py:479

commit v9 on v8

--- a/solution.py
+++ b/solution.py
@@ -71,6 +71,8 @@
 ORDER = [7, 6, 8, 4, 1, 3, 5, 0, 2]
 
 
+SHARED = [3, 5, 4, 6, 8]
+UNSHARED = [1, 0, 2]
 FAR_FIRST = (4, 5, 3, 6, 2, 7, 1, 0)
 
 
@@ -93,7 +95,7 @@
                  squares, x_ref, cot_ref, gain_first_ref, gain_second_ref, bias_ref, k1, k2, k1t, k2t, x_cells, h_cells, d_cells,
                  left, cells, packed,
                  core_in, part, x_out, x_in, y_out, y_in, z_in, vz, vy, vx, vc,
-                 local_sem, hx_sem, hc_sem, hh_sem,
+                 local_sem, hx_sem, hc_sem, hh_sem, relay_sem,
                  core_sem, x_sem, y_sem, z_sem, gy_sem, gx_sem, gc_sem,
                  vz_sem, vy_sem, vx_sem, vc_sem):
     tm, row = lax.axis_index("tm"), lax.axis_index("row")
@@ -127,11 +129,14 @@
         p, q = CELLS[cell]
         return {"tm": lax.rem(tm + 6 + p, 8), "row": lax.rem(row + 63 + q, 64)}
 
-    def send(src, dst, sems, slot, device):
-        copy = pltpu.make_async_remote_copy(
+    def remote(src, dst, sems, slot, device):
+        return pltpu.make_async_remote_copy(
             src_ref=src, dst_ref=dst, send_sem=sems.at[0, slot], recv_sem=sems.at[1, slot],
             device_id=device, device_id_type=MESH,
         )
+
+    def send(src, dst, sems, slot, device):
+        copy = remote(src, dst, sems, slot, device)
         copy.start()
         return copy
 
@@ -155,9 +160,26 @@
     sent = []
     x_copies, c_copies = {}, {}
     for cell in halo:
-        x_copies[cell] = send(x_ref, x_cells.at[cell], hx_sem, cell, later(cell))
-        c_copies[cell] = send(cot_ref, cells.at[1, band_of(cell)], hc_sem, cell, earlier(cell))
-    sent += list(x_copies.values()) + list(c_copies.values())
+        x_copies[cell] = remote(x_ref, x_cells.at[cell], hx_sem, cell, later(cell))
+        c_copies[cell] = remote(
+            cot_ref, cells.at[1, band_of(cell)], hc_sem, cell, earlier(cell)
+        )
+
+    def each_sent(act, here):
+        for cell in SHARED:
+            p, q = CELLS[cell]
+            if here == 1 or (p, q) == (1, 1) or p == 2:
+                act(x_copies[cell])
+            if here == 0 or (p, q) == (1, 1) or p == 2:
+                act(c_copies[cell])
+        for cell in UNSHARED:
+            act((x_copies if here == 0 else c_copies)[cell])
+
+    for here in (0, 1):
+
+        @pl.when(me_c == here)
+        def _():
+            each_sent(lambda copy: copy.start(), here)
 
     for load in loads[2:]:
         load.wait()
@@ -185,17 +207,58 @@
         p, q = CELLS[cell]
         return (tm + 2 - p <= 7) & (row + 1 - q >= 0) & (row + 1 - q <= 63)
 
+    def take_x(cell):
+        x_copies[cell].wait_recv()
+
+        @pl.when(jnp.logical_not(before(cell)))
+        def _():
+            x_cells[cell] = jnp.zeros((C, W), bf16)
+
+    def take_c(cell):
+        c_copies[cell].wait_recv()
+
+        @pl.when(jnp.logical_not(after(cell)))
+        def _():
+            cells[1, band_of(cell), :] = jnp.zeros((C, W), bf16)
+
+    def relay(src, dst, sems, relay_sem, n, cell):
+        return pltpu.make_async_remote_copy(
+            src_ref=src, dst_ref=dst, send_sem=relay_sem.at[n], recv_sem=sems.at[1, cell - 3],
+            device_id=peer_c, device_id_type=MESH,
+        )
+
+    x_relays = [
+        relay(x_cells.at[cell], x_cells.at[cell - 3], hx_sem, relay_sem, n, cell)
+        for n, cell in enumerate(SHARED)
+    ]
+    c_relays = [
+        relay(
+            cells.at[1, band_of(cell)], cells.at[1, band_of(cell - 3)], hc_sem, relay_sem, n, cell
+        )
+        for n, cell in enumerate(SHARED)
+    ]
+
+    @pl.when(me_c == 0)
+    def _():
+        for n, cell in enumerate(SHARED):
+            take_x(cell)
+            x_relays[n].start()
+
+    @pl.when(me_c == 1)
+    def _():
+        for n, cell in enumerate(SHARED):
+            take_c(cell)
+            c_relays[n].start()
+
     sums = jnp.zeros((3 * C, W), f32)
     for cell in ORDER:
         if cell == OWN:
             wide = x_ref[...].astype(f32)
         else:
-            x_copies[cell].wait_recv()
-
-            @pl.when(jnp.logical_not(before(cell)))
-            def _():
-                x_cells[cell] = jnp.zeros((C, W), bf16)
-
+            if cell in SHARED:
+                pl.when(me_c == 1)(lambda cell=cell: take_x(cell))
+            else:
+                take_x(cell)
             wide = x_cells[cell].astype(f32)
         value, slope, unit, inverse = act_parts(wide, gain_first)
         if cell == OWN:
@@ -215,11 +278,10 @@
     sums = jnp.zeros((3 * C, W), f32)
     for cell in ORDER:
         if cell != OWN:
-            c_copies[cell].wait_recv()
-
-            @pl.when(jnp.logical_not(after(cell)))
-            def _():
-                cells[1, band_of(cell), :] = jnp.zeros((C, W), bf16)
+            if cell in SHARED:
+                pl.when(me_c == 0)(lambda cell=cell: take_c(cell))
+            else:
+                take_c(cell)
 
         sums = sums + dot_nn(k2t[cell], cells[1, band_of(cell), :])
     grad_second = shift_columns(sums[:C], 1) + sums[C : 2 * C] + shift_columns(sums[2 * C :], -1)
@@ -241,17 +303,17 @@
     for k, d in enumerate(FAR_FIRST):
         core_copies.append(send(packed.at[1 - me_c, :, at_y(d)], core_in.at[k], core_sem, k, peer_c))
     put_rows(packed, me_c, dot_nt(left[me_c], cells[me_c]))
-    x_copies = []
+    xs_copies = []
     for k, d in enumerate(FAR_FIRST):
         core_copies[k].wait_recv()
         total = packed[me_c, :, at_y(d)] + core_in[k]
         x_out[k] = total.astype(bf16)
         part[k] = packed[me_c, me_x, at_y(d)] + core_in[k, me_x]
         for e in (2, 1, 3):
-            x_copies.append(
+            xs_copies.append(
                 send(x_out.at[k, at_x(e)], x_in.at[k, e - 1], x_sem, k * 3 + e - 1, peer_x(e))
             )
-    sent += core_copies + x_copies
+    sent += core_copies + xs_copies
 
     h_copies = {}
     for cell in halo:
@@ -280,7 +342,7 @@
     y_copies = []
     for k, d in enumerate(FAR_FIRST):
         total = part[k]
-        for copy in x_copies[3 * k : 3 * k + 3]:
+        for copy in xs_copies[3 * k : 3 * k + 3]:
             copy.wait_recv()
         for e in range(3):
             total = total + x_in[k, e].astype(f32)
@@ -301,6 +363,14 @@
     for copy in sent:
         copy.wait_send()
     sent = []
+    for here in (0, 1):
+
+        @pl.when(me_c == here)
+        def _():
+            each_sent(lambda copy: copy.wait_send(), here)
+            for copy in (x_relays, c_relays)[here]:
+                copy.wait_send()
+
     sums = dot_nn(k1t[OWN], left[0, h_own, :])
     for cell in ORDER[1:]:
         h_copies[cell].wait_recv()
@@ -458,7 +528,7 @@
             vmem((8, 64, LANES), bf16),
             vmem((8, 8, LANES), f32), vmem((8, 8, LANES), f32),
             vmem((4, 8, LANES), f32), vmem((2, 8, LANES), f32),
-            dma((7,)), dma((2, 9)), dma((2, 9)), dma((2, 9)),
+            dma((7,)), dma((2, 9)), dma((2, 9)), dma((2, 9)), dma((5,)),
             dma((2, 8)), dma((2, 24)), dma((2, 7)), dma((2, 7)),
             dma((2, 7)), dma((2, 24)), dma((2, 32)),
             dma((2, 7)), dma((2, 7)), dma((2, 3)), dma((2, 1)),

time: 64.4 us -> 61.8 us (0.960)
  Pallas kernels: 63.6 us -> 61 us
    pallas_call x1, Pallas kernels: 61.2 us -> 58.6 us  [body(): pl.pallas_call(block_kernel, out_shape=(jax.ShapeDtypeStruct((2, 4, 8, 64...]
where the time goes in v9:
time: 61.8 us; the launch traced here: 61.7 us
  Pallas kernels  61 us (99%)
  between operations  0.64 us (1%)
    pallas_call x1, Pallas kernels, body(): pl.pallas_call(block_kernel, out_shape=(jax.ShapeDtypeStruct((2, 4, 8, 64...  58.6 us
    pallas_call x1, Pallas kernels, body(): pl.pallas_call(scale_kernel, out_shape=(jax.ShapeDtypeStruct((9, 3 * C, C...  2.45 us

profile of v9, /device:TPU:1, one launch (start us, length us, event | category | flops | bytes accessed | tf_op | source)
XLA Modules:
  0.0 61.7 jit_solution(12711464285714685627)
XLA Ops:
  0.6 58.6 %shard_map.102 = (bf16[2,4,8,64,128]{4,3,2,1,0:T(8,128)(2,1)S(1)}, f32[16,128]{1,0:T(8,128)S(1)}, bf16[96,256]{1,0:T(8,128)(2,1)S(1)}) custom-call(bf16[96,256]{1,0:T(8,128)(2,1)} %bitcast.14, bf16[96,256]{1,0:T(8,128)(2,1)} %bitcast.15, f32[1,96]{1,0:T(1,128)} %bitcast.16, f32[1,96]{1,0:T(1,128)} %bitcast.17, f32[1,96]{1,0:T(1,128)} %bitcast.18, ...), custom_call_target="tpu_custom_call" | custom-call | tf_op jit(solution)/shard_map/pallas_call | solution.py:504
  59.2 2.5 %shard_map.103 = (f32[9,288,96]{2,1,0:T(8,128)}, f32[9,288,96]{2,1,0:T(8,128)}, f32[4,96]{1,0:T(4,128)}, bf16[96,256]{1,0:T(8,128)(2,1)}) custom-call(bf16[4096,128]{1,0:T(8,128)(2,1)S(1)} %bitcast.11, f32[16,128]{1,0:T(8,128)S(1)} %get-tuple-element.12.stats_ref, bf16[96,256]{1,0:T(8,128)(2,1)S(1)} %get-tuple-element.13.grad_in_ref), custom_call_target="tpu_custom_call" | custom-call | tf_op jit(solution)/shard_map/pallas_call | solution.py:549

commit v10 on v9

--- a/solution.py
+++ b/solution.py
@@ -95,7 +95,7 @@
                  squares, x_ref, cot_ref, gain_first_ref, gain_second_ref, bias_ref, k1, k2, k1t, k2t, x_cells, h_cells, d_cells,
                  left, cells, packed,
                  core_in, part, x_out, x_in, y_out, y_in, z_in, vz, vy, vx, vc,
-                 local_sem, hx_sem, hc_sem, hh_sem, relay_sem,
+                 local_sem, hx_sem, hc_sem, hh_sem, relay_sem, h_relay_sem,
                  core_sem, x_sem, y_sem, z_sem, gy_sem, gx_sem, gc_sem,
                  vz_sem, vy_sem, vx_sem, vc_sem):
     tm, row = lax.axis_index("tm"), lax.axis_index("row")
@@ -317,7 +317,30 @@
 
     h_copies = {}
     for cell in halo:
-        h_copies[cell] = send(left.at[0, h_own], h_cells.at[cell], hh_sem, cell, earlier(cell))
+        h_copies[cell] = remote(left.at[0, h_own], h_cells.at[cell], hh_sem, cell, earlier(cell))
+    h_relays = [
+        pltpu.make_async_remote_copy(
+            src_ref=h_cells.at[cell], dst_ref=h_cells.at[cell - 3],
+            send_sem=h_relay_sem.at[n], recv_sem=hh_sem.at[1, cell - 3],
+            device_id=peer_c, device_id_type=MESH,
+        )
+        for n, cell in enumerate(SHARED)
+    ]
+
+    def each_hidden(act, here):
+        for cell in SHARED:
+            p, q = CELLS[cell]
+            if here == 0 or (p, q) == (1, 1) or p == 2:
+                act(h_copies[cell])
+        if here == 1:
+            for cell in UNSHARED:
+                act(h_copies[cell])
+
+    for here in (0, 1):
+
+        @pl.when(me_c == here)
+        def _():
+            each_hidden(lambda copy: copy.start(), here)
 
     gained = jnp.zeros((3 * C, C), f32)
     for cell in range(9):
@@ -371,20 +394,30 @@
             for copy in (x_relays, c_relays)[here]:
                 copy.wait_send()
 
-    sums = dot_nn(k1t[OWN], left[0, h_own, :])
-    for cell in ORDER[1:]:
+    def take_h(cell):
         h_copies[cell].wait_recv()
 
         @pl.when(jnp.logical_not(after(cell)))
         def _():
             h_cells[cell] = jnp.zeros((C, W), bf16)
 
+    @pl.when(me_c == 1)
+    def _():
+        for n, cell in enumerate(SHARED):
+            take_h(cell)
+            h_relays[n].start()
+
+    sums = dot_nn(k1t[OWN], left[0, h_own, :])
+    for cell in ORDER[1:]:
+        if cell in SHARED:
+            pl.when(me_c == 0)(lambda cell=cell: take_h(cell))
+        else:
+            take_h(cell)
         sums = sums + dot_nn(k1t[cell], h_cells[cell])
     grad_first = shift_columns(sums[:C], 1) + sums[C : 2 * C] + shift_columns(sums[2 * C :], -1)
     input_term = back_through_norm(grad_first * own_slope, gain_first, own_unit, own_inverse)
     grad_in_ref[...] = (c_own.astype(f32) + input_term).astype(bf16)
 
-    sent += list(h_copies.values())
     vx[me_x] = vector_total(vy, 8)
     v_copies = [send(vx.at[me_x], vx.at[me_x], vx_sem, d - 1, peer_x(d)) for d in range(1, 4)]
     for copy in z_copies:
@@ -436,6 +469,15 @@
         if k == 0:
             vc[me_c] = vector_total(vx, 4)
             v_copies = [send(vc.at[me_c], vc.at[me_c], vc_sem, 0, peer_c)]
+    for here in (0, 1):
+
+        @pl.when(me_c == here)
+        def _():
+            each_hidden(lambda copy: copy.wait_send(), here)
+            if here == 1:
+                for copy in h_relays:
+                    copy.wait_send()
+
     for copy in sent:
         copy.wait_send()
     sent = list(gy_copies.values()) + list(gx_copies.values()) + gc_copies
@@ -528,7 +570,7 @@
             vmem((8, 64, LANES), bf16),
             vmem((8, 8, LANES), f32), vmem((8, 8, LANES), f32),
             vmem((4, 8, LANES), f32), vmem((2, 8, LANES), f32),
-            dma((7,)), dma((2, 9)), dma((2, 9)), dma((2, 9)), dma((5,)),
+            dma((7,)), dma((2, 9)), dma((2, 9)), dma((2, 9)), dma((5,)), dma((5,)),
             dma((2, 8)), dma((2, 24)), dma((2, 7)), dma((2, 7)),
             dma((2, 7)), dma((2, 24)), dma((2, 32)),
             dma((2, 7)), dma((2, 7)), dma((2, 3)), dma((2, 1)),

time: 61.8 us -> 61.2 us (level)
  no operation moved by 1% of the time
where the time goes in v10:
time: 61.2 us; the launch traced here: 61.1 us
  Pallas kernels  60.5 us (99%)
  between operations  0.64 us (1%)
    pallas_call x1, Pallas kernels, body(): pl.pallas_call(block_kernel, out_shape=(jax.ShapeDtypeStruct((2, 4, 8, 64...  58 us
    pallas_call x1, Pallas kernels, body(): pl.pallas_call(scale_kernel, out_shape=(jax.ShapeDtypeStruct((9, 3 * C, C...  2.44 us

profile of v10, /device:TPU:1, one launch (start us, length us, event | category | flops | bytes accessed | tf_op | source)
XLA Modules:
  0.0 61.1 jit_solution(5200736065964750397)
XLA Ops:
  0.6 58.0 %shard_map.102 = (bf16[2,4,8,64,128]{4,3,2,1,0:T(8,128)(2,1)S(1)}, f32[16,128]{1,0:T(8,128)S(1)}, bf16[96,256]{1,0:T(8,128)(2,1)S(1)}) custom-call(bf16[96,256]{1,0:T(8,128)(2,1)} %bitcast.14, bf16[96,256]{1,0:T(8,128)(2,1)} %bitcast.15, f32[1,96]{1,0:T(1,128)} %bitcast.16, f32[1,96]{1,0:T(1,128)} %bitcast.17, f32[1,96]{1,0:T(1,128)} %bitcast.18, ...), custom_call_target="tpu_custom_call" | custom-call | tf_op jit(solution)/shard_map/pallas_call | solution.py:546
  58.7 2.4 %shard_map.103 = (f32[9,288,96]{2,1,0:T(8,128)}, f32[9,288,96]{2,1,0:T(8,128)}, f32[4,96]{1,0:T(4,128)}, bf16[96,256]{1,0:T(8,128)(2,1)}) custom-call(bf16[4096,128]{1,0:T(8,128)(2,1)S(1)} %bitcast.11, f32[16,128]{1,0:T(8,128)S(1)} %get-tuple-element.12.stats_ref, bf16[96,256]{1,0:T(8,128)(2,1)S(1)} %get-tuple-element.13.grad_in_ref), custom_call_target="tpu_custom_call" | custom-call | tf_op jit(solution)/shard_map/pallas_call | solution.py:591
